TPU v7x, 128 devices: a whole 4x4x4 slice. The times are simulated.
128 devices in a mesh: dp: 4 (over x_hi, core), seq: 32 (over x_lo, y, z).
Axes of the slice: x: 4 (x_hi: 2, x_lo: 2; x = x_hi * 2 + x_lo), y: 4, z: 4, core: 2. Of those that a mesh axis runs over, the one named last changes fastest.
Arguments:
- hidden: bfloat16 [4, 4096, 2432], P('dp', 'seq'), may hold values from -6 to 6
- out_cot: bfloat16 [4, 4096, 2432], P('dp', 'seq'), may hold values from -6 to 6
- proj_in: bfloat16 [2432, 4096], P(None, 'dp'), may hold values from -0.125 to 0.125
- proj_out: bfloat16 [4096, 1536], P('dp'), may hold values from -0.09375 to 0.09375
- attn_out_w: bfloat16 [2048, 2432], replicated, may hold values from -0.125 to 0.125
- queries: bfloat16 [4, 4096, 2048], P('dp', 'seq'), as said below
- keys: bfloat16 [4, 4096, 2048], P('dp', 'seq'), as said below
- values: bfloat16 [4, 4096, 2048], P('dp', 'seq'), may hold values from -6 to 6
- dino: bfloat16 [4, 1536, 4096], P('dp', 'seq'), as said below
Outputs:
- cosine: float32 [4, 4096], P('dp', 'seq')
- grad_queries: bfloat16 [4, 4096, 2048], P('dp', 'seq')
- grad_keys: bfloat16 [4, 4096, 2048], P('dp', 'seq')
- grad_values: bfloat16 [4, 4096, 2048], P('dp', 'seq')
Inputs may be any that keep to these rules, and one draw needn't show every extreme that they name: `dino`: real-valued features, channels of differing scale and offset. real-valued queries. real-valued keys.
All inputs are finite; a program needn't handle non-finite values.
Results may differ from a plain program's by a relative error of at most 0.014.
Values may be sent and summed in bfloat16 or wider, within the bound.
A program may use at most 128 MiB of HBM per device.

v0:
```python
import jax
import jax.numpy as jnp
from jax import lax
from jax.sharding import PartitionSpec as P

HEAD_DIM = 64


loss_weight = 1000.0


def unit_target(features):
    values32 = features.astype(jnp.float32)
    center = jnp.mean(values32, axis=1, keepdims=True)
    shifted = values32 - center
    spread = jnp.mean(shifted * shifted, axis=1, keepdims=True)
    normed = shifted * lax.rsqrt(spread + 1e-06)
    unit = normed * lax.rsqrt(jnp.sum(normed * normed, axis=1, keepdims=True) + 1e-06)
    return jnp.transpose(unit, (0, 2, 1))


def cosine_grad(projected, target):
    rinv = lax.rsqrt(jnp.sum(projected * projected, axis=-1, keepdims=True) + 1e-06)
    direction = projected * rinv
    cosine = jnp.sum(direction * target, axis=-1)
    grad_z = -loss_weight * rinv * (target - cosine[..., None] * direction)
    return (cosine, grad_z.astype(jnp.bfloat16))


def silu_slope(pre_act):
    sigma = jax.nn.sigmoid(pre_act)
    return sigma * (1.0 + pre_act * (1.0 - sigma))


def attention_backward(heads_q, heads_k, heads_v, heads_g):
    length = heads_q.shape[1]
    per_dev = heads_q.shape[2] // HEAD_DIM
    scale = HEAD_DIM ** (-0.5)
    block = min(512, length)
    blocks = length // block
    key_rows = heads_k.reshape(length, per_dev, HEAD_DIM)
    value_rows = heads_v.reshape(length, per_dev, HEAD_DIM)
    query_blocks = heads_q.reshape(blocks, block, per_dev, HEAD_DIM)
    grad_blocks = heads_g.reshape(blocks, block, per_dev, HEAD_DIM)

    def visit(carry, item):
        acc_keys, acc_values = carry
        query_blk, grad_blk = item
        scores = (
            jnp.einsum("qhd,khd->hqk", query_blk, key_rows, preferred_element_type=jnp.float32)
            * scale
        )
        probs = jax.nn.softmax(scores, axis=-1)
        probs_b = probs.astype(jnp.bfloat16)
        attended = jnp.einsum(
            "hqk,khd->qhd", probs_b, value_rows, preferred_element_type=jnp.float32
        )
        row_dot = jnp.einsum("qhd,qhd->hq", grad_blk.astype(jnp.float32), attended)
        grad_p = jnp.einsum(
            "qhd,khd->hqk", grad_blk, value_rows, preferred_element_type=jnp.float32
        )
        grad_s = (probs * (grad_p - row_dot[:, :, None])).astype(jnp.bfloat16)
        grad_qblk = (
            jnp.einsum("hqk,khd->qhd", grad_s, key_rows, preferred_element_type=jnp.float32) * scale
        ).astype(jnp.bfloat16)
        acc_keys = acc_keys + jnp.einsum(
            "hqk,qhd->khd", grad_s, query_blk, preferred_element_type=jnp.float32
        )
        acc_values = acc_values + jnp.einsum(
            "hqk,qhd->khd", probs_b, grad_blk, preferred_element_type=jnp.float32
        )
        return ((acc_keys, acc_values), grad_qblk)

    zeros_acc = jnp.zeros((length, per_dev, HEAD_DIM), jnp.float32)
    (acc_keys, acc_values), grad_query = lax.scan(
        visit, (zeros_acc, zeros_acc), (query_blocks, grad_blocks)
    )
    grad_q = grad_query.reshape(1, length, per_dev * HEAD_DIM)
    grad_k = (acc_keys * scale).astype(jnp.bfloat16).reshape(1, length, per_dev * HEAD_DIM)
    grad_v = acc_values.astype(jnp.bfloat16).reshape(1, length, per_dev * HEAD_DIM)
    return (grad_q, grad_k, grad_v)


def on_device(hidden, out_cot, proj_in, proj_out, attn_out_w, queries, keys, values, dino):
    features = lax.all_to_all(dino, "seq", split_axis=2, concat_axis=1, tiled=True)
    target = unit_target(features)
    pre_act = jnp.einsum(
        "itd,dh->ith",
        lax.all_gather(hidden, "dp", axis=0, tiled=True),
        proj_in,
        preferred_element_type=jnp.float32,
    )
    silu_out = jax.nn.silu(pre_act).astype(jnp.bfloat16)
    picked = silu_out
    projected = lax.psum_scatter(
        jnp.einsum("ith,hc->itc", picked, proj_out, preferred_element_type=jnp.float32),
        "dp",
        scatter_dimension=0,
        tiled=True,
    )
    cosine, grad_z = cosine_grad(projected, target)
    grad_silu = jnp.einsum(
        "itc,hc->ith",
        lax.all_gather(grad_z, "dp", axis=0, tiled=True),
        proj_out,
        preferred_element_type=jnp.float32,
    )
    grad_pre = (grad_silu * silu_slope(pre_act)).astype(jnp.bfloat16)
    picked = grad_pre
    grad_repa = lax.psum_scatter(
        jnp.einsum("ith,dh->itd", picked, proj_in, preferred_element_type=jnp.float32),
        "dp",
        scatter_dimension=0,
        tiled=True,
    )
    grad_hidden = (out_cot.astype(jnp.float32) + grad_repa).astype(jnp.bfloat16)
    grad_attn = jnp.einsum(
        "itd,ed->ite", grad_hidden, attn_out_w, preferred_element_type=jnp.float32
    ).astype(jnp.bfloat16)
    heads_q, heads_k, heads_v, heads_g = (
        lax.all_to_all(queries, "seq", split_axis=2, concat_axis=1, tiled=True),
        lax.all_to_all(keys, "seq", split_axis=2, concat_axis=1, tiled=True),
        lax.all_to_all(values, "seq", split_axis=2, concat_axis=1, tiled=True),
        lax.all_to_all(grad_attn, "seq", split_axis=2, concat_axis=1, tiled=True),
    )
    grad_q, grad_k, grad_v = attention_backward(heads_q, heads_k, heads_v, heads_g)
    back_q, back_k, back_v = (
        lax.all_to_all(grad_q, "seq", split_axis=1, concat_axis=2, tiled=True),
        lax.all_to_all(grad_k, "seq", split_axis=1, concat_axis=2, tiled=True),
        lax.all_to_all(grad_v, "seq", split_axis=1, concat_axis=2, tiled=True),
    )
    return (cosine, back_q, back_k, back_v)


def solution(mesh):
    in_specs = (
        P("dp", "seq", None),
        P("dp", "seq", None),
        P(None, "dp"),
        P("dp", None),
        P(),
        P("dp", "seq", None),
        P("dp", "seq", None),
        P("dp", "seq", None),
        P("dp", "seq", None),
    )
    out_specs = (P("dp", "seq"), P("dp", "seq", None), P("dp", "seq", None), P("dp", "seq", None))
    return jax.shard_map(
        on_device, mesh=mesh, in_specs=in_specs, out_specs=out_specs, check_vma=False
    )
```

profile of v0, /device:TPU:0, one launch (start us, length us, event | category | flops | bytes accessed | tf_op | source)
XLA Modules:
  0.0 640.4 jit_solution(1516484496861264055)
XLA Ops:
  8.0 33.1 %all-gather.3.cloned.1.call-done = bf16[4,128,2432]{2,1,0:T(8,128)(2,1)} async-done(((bf16[1,128,2432]{2,1,0:T(8,128)(2,1)}), bf16[4,128,2432]{2,1,0:T(8,128)(2,1)}) %all-gather.3.cloned.1.call-update) | async-done | bytes 2490384 | tf_op jit(solution)/shard_map/all_gather | solution.py:89
  41.0 5.5 fusion.35
  56.8 24.4 %reduce.19 = bf16[4096,48]{1,0:T(8,128)(2,1)} reduce(bf16[4096,1,48]{2,1,0:T(2,128)(2,1)} %bitcast.204, bf16[]{:T(256)} %broadcast.188), dimensions={1}, to_apply=%bitcast.141.reduce_sub_computation | reduce | bytes 786434
  85.0 18.1 %all_to_all.123 = bf16[32,2,3072]{2,1,0:T(2,128)(2,1)S(1)} all-to-all(bf16[32,2,3072]{2,1,0:T(2,128)(2,1)} %reshape.308), channel_id=1, replica_groups=mesh['dp'=4,'seq'=32] {'seq'}, dimensions={0} | all-to-all | bytes 786432 | tf_op jit(solution)/shard_map/all_to_all | solution.py:85
  107.1 5.8 copy.110
  117.7 31.6 %convert_reduce_fusion = f32[4096]{0:T(1024)S(1)} fusion(bf16[4096,1,48]{2,1,0:T(2,128)(2,1)} %reshape.309), kind=kLoop, calls=%fused_computation.69 | loop fusion | flops 389120 | bytes 409600 | tf_op jit(solution)/shard_map/reduce_sum | solution.py:14
  157.1 20.6 %all-gather.5.cloned.1.call-done = bf16[4,128,1536]{2,1,0:T(8,128)(2,1)} async-done(((bf16[1,128,1536]{2,1,0:T(8,128)(2,1)}), bf16[4,128,1536]{2,1,0:T(8,128)(2,1)}) %all-gather.5.cloned.1.call-update) | async-done | bytes 1572880 | tf_op jit(solution)/shard_map/all_gather | solution.py:104
  177.7 10.5 %fusion.33 = f32[4,128,2432]{2,1,0:T(8,128)} fusion(bf16[2432,1024]{1,0:T(8,128)(2,1)} %param.13, f32[4,128,1024]{2,1,0:T(8,128)} %copy-done.13, bf16[4,128,1536]{2,1,0:T(8,128)(2,1)} %all-gather.5.cloned.1.call-done, bf16[1024,1536]{1,0:T(8,128)(2,1)S(1)} %copy-done), kind=kOutput, calls=%fused_computation.35 | convolution fusion | flops 4165468160 | bytes 16777216 | tf_op jit(solution)/shard_map/ith,dh->itd/dot_general | solution.py:111
  190.0 11.5 %reduce.20 = bf16[2048,128]{1,0:T(8,128)(2,1)S(1)} reduce(bf16[2048,1,128]{2,1,0:T(2,128)(2,1)S(1)} %bitcast.211, bf16[]{:T(256)} %broadcast.188), dimensions={1}, to_apply=%bitcast.143.reduce_sub_computation | reduce | bytes 1048578
  202.4 7.8 %all-to-all-start.1 = ((bf16[32,2,4096]{2,1,0:T(2,128)(2,1)}), bf16[32,2,4096]{2,1,0:T(2,128)(2,1)S(1)}, u32[]{:S(2)}, u32[]{:S(2)}) async-start(bf16[32,2,4096]{2,1,0:T(2,128)(2,1)} %reshape.310), calls=%async_computation.2 | async-start | bytes 1048576 | tf_op jit(solution)/shard_map/all_to_all | solution.py:121
  211.0 11.5 %reduce.21 = bf16[2048,128]{1,0:T(8,128)(2,1)S(1)} reduce(bf16[2048,1,128]{2,1,0:T(2,128)(2,1)S(1)} %bitcast.212, bf16[]{:T(256)} %broadcast.188), dimensions={1}, to_apply=%bitcast.145.reduce_sub_computation | reduce | bytes 1048578
  225.3 6.5 %all-to-all-start.2 = ((bf16[32,2,4096]{2,1,0:T(2,128)(2,1)}), bf16[32,2,4096]{2,1,0:T(2,128)(2,1)S(1)}, u32[]{:S(2)}, u32[]{:S(2)}) async-start(bf16[32,2,4096]{2,1,0:T(2,128)(2,1)} %reshape.312), calls=%async_computation.3 | async-start | bytes 1048576 | tf_op jit(solution)/shard_map/all_to_all | solution.py:122
  232.6 11.5 %reduce.23 = bf16[2048,128]{1,0:T(8,128)(2,1)S(1)} reduce(bf16[2048,1,128]{2,1,0:T(2,128)(2,1)S(1)} %bitcast.213, bf16[]{:T(256)} %broadcast.188), dimensions={1}, to_apply=%bitcast.149.reduce_sub_computation | reduce | bytes 1048578
  253.6 7.7 %fusion.41 = bf16[1,128,2048]{2,1,0:T(8,128)(2,1)S(1)} fusion(bf16[2048,2432]{1,0:T(8,128)(2,1)} %param.15, f32[1,128,2432]{2,1,0:T(8,128)} %reduce-scatter.5.cloned.1.call-done, bf16[1,128,2432]{2,1,0:T(8,128)(2,1)} %param.12), kind=kOutput, calls=%fused_computation.44 | convolution fusion | flops 1276264448 | bytes 12353536 | tf_op jit(solution)/shard_map/itd,ed->ite/dot_general | solution.py:117
  262.1 11.5 %reduce.22 = bf16[2048,128]{1,0:T(8,128)(2,1)S(1)} reduce(bf16[2048,1,128]{2,1,0:T(2,128)(2,1)S(1)} %bitcast.210, bf16[]{:T(256)} %broadcast.188), dimensions={1}, to_apply=%bitcast.147.reduce_sub_computation | reduce | bytes 1048578
  274.5 8.6 %all-to-all-start.3 = ((bf16[32,2,4096]{2,1,0:T(2,128)(2,1)}), bf16[32,2,4096]{2,1,0:T(2,128)(2,1)}, u32[]{:S(2)}, u32[]{:S(2)}) async-start(bf16[32,2,4096]{2,1,0:T(2,128)(2,1)} %reshape.314), calls=%async_computation.5 | async-start | bytes 1048576 | tf_op jit(solution)/shard_map/all_to_all | solution.py:124
  311.9 182.4 %while.15 = (s32[]{:T(128)}, f32[4096,1,64]{0,2,1:T(8,128)S(1)}, f32[4096,1,64]{0,2,1:T(8,128)S(1)}, bf16[8,512,1,64]{1,3,2,0:T(8,128)(2,1)}, bf16[8,512,1,64]{1...) while((s32[]{:T(128)}, f32[4096,1,64]{0,2,1:T(8,128)S(1)}, ...), condition=%wide.region_11.12_spmd.clone, body=%wide.region_8.11_spmd.clone.sunk | while | flops 1639086592 | bytes 145113792 | solution.py:75
  498.0 22.6 %reduce.26 = bf16[4096,64]{1,0:T(8,128)(2,1)S(1)} reduce(bf16[4096,1,64]{2,1,0:T(2,128)(2,1)S(1)} %bitcast.202, bf16[]{:T(256)} %broadcast.188), dimensions={1}, to_apply=%bitcast.155.reduce_sub_computation | reduce | bytes 1048578
  522.1 8.8 %all-to-all-start.7 = ((bf16[32,2,4096]{2,1,0:T(2,128)(2,1)}), bf16[32,2,4096]{2,1,0:T(2,128)(2,1)}, u32[]{:S(2)}, u32[]{:S(2)}) async-start(bf16[32,2,4096]{2,1,0:T(2,128)(2,1)} %reshape.322), calls=%async_computation.9 | async-start | bytes 1048576 | tf_op jit(solution)/shard_map/all_to_all | solution.py:130
  535.9 22.4 %reduce.25 = bf16[4096,64]{1,0:T(8,128)(2,1)S(1)} reduce(bf16[4096,1,64]{2,1,0:T(2,128)(2,1)S(1)} %bitcast.203, bf16[]{:T(256)} %broadcast.188), dimensions={1}, to_apply=%bitcast.153.reduce_sub_computation | reduce | bytes 1048578
  559.8 8.7 %all-to-all-start.6 = ((bf16[32,2,4096]{2,1,0:T(2,128)(2,1)}), bf16[32,2,4096]{2,1,0:T(2,128)(2,1)}, u32[]{:S(2)}, u32[]{:S(2)}) async-start(bf16[32,2,4096]{2,1,0:T(2,128)(2,1)} %reshape.320), calls=%async_computation.8 | async-start | bytes 1048576 | tf_op jit(solution)/shard_map/all_to_all | solution.py:129
  570.6 22.4 %reduce.24 = bf16[4096,64]{1,0:T(8,128)(2,1)S(1)} reduce(bf16[4096,1,64]{2,1,0:T(2,128)(2,1)S(1)} %bitcast.205, bf16[]{:T(256)} %broadcast.188), dimensions={1}, to_apply=%bitcast.151.reduce_sub_computation | reduce | bytes 1048578
  594.5 8.6 %all-to-all-start.5 = ((bf16[32,2,4096]{2,1,0:T(2,128)(2,1)}), bf16[32,2,4096]{2,1,0:T(2,128)(2,1)}, u32[]{:S(2)}, u32[]{:S(2)}) async-start(bf16[32,2,4096]{2,1,0:T(2,128)(2,1)} %reshape.318), calls=%async_computation.7 | async-start | bytes 1048576 | tf_op jit(solution)/shard_map/all_to_all | solution.py:128
  618.5 5.7 reshape.319
  (206 shorter events, 300.1 us)
Async XLA Ops:
  7.2 40.7 %copy-start = (bf16[1024,1536]{1,0:T(8,128)(2,1)S(1)}, bf16[1024,1536]{1,0:T(8,128)(2,1)}, u32[]{:S(2)}) copy-start(bf16[1024,1536]{1,0:T(8,128)(2,1)} %param.14) | copy-start | bytes 9437188
  7.2 33.8 %all-gather.3.cloned.1.call-start = ((), (), s32[]{:S(2)}) async-start(), calls=%async_computation.10 | async-start | bytes 3112960 | tf_op jit(solution)/shard_map/all_gather | solution.py:89
  7.9 143.0 %reduce-scatter.3.cloned.1.call-start = ((), (), s32[]{:S(2)}) async-start(), calls=%async_computation.11 | async-start | bytes 3932160 | tf_op jit(solution)/shard_map/reduce_scatter | solution.py:95
  51.4 126.3 %all-gather.5.cloned.1.call-start = ((), (), s32[]{:S(2)}) async-start(), calls=%async_computation.12 | async-start | bytes 1966080 | tf_op jit(solution)/shard_map/all_gather | solution.py:104
  117.7 33.0 %copy-start.4 = (f32[1,48,4096]{2,0,1:T(1,128)S(1)}, f32[1,48,4096]{2,0,1:T(1,128)}, u32[]{:S(2)}) copy-start(f32[1,48,4096]{2,0,1:T(1,128)} %copy.110) | copy-start | bytes 2359300
  156.8 96.8 %reduce-scatter.5.cloned.1.call-start = ((), (), s32[]{:S(2)}) async-start(), calls=%async_computation.13 | async-start | bytes 6225920 | tf_op jit(solution)/shard_map/reduce_scatter | solution.py:110
  189.3 21.0 %copy-start.9 = (bf16[1,128,2048]{2,1,0:T(8,128)(2,1)S(1)}, bf16[1,128,2048]{2,1,0:T(8,128)(2,1)}, u32[]{:S(2)}) copy-start(bf16[1,128,2048]{2,1,0:T(8,128)(2,1)} %param.17) | copy-start | bytes 1572868
  202.4 29.4 %copy-start.10 = (bf16[1,128,2048]{2,1,0:T(8,128)(2,1)S(1)}, bf16[1,128,2048]{2,1,0:T(8,128)(2,1)}, u32[]{:S(2)}) copy-start(bf16[1,128,2048]{2,1,0:T(8,128)(2,1)} %param.18) | copy-start | bytes 1572868
  202.4 22.9 %all-to-all-start.1 = ((bf16[32,2,4096]{2,1,0:T(2,128)(2,1)}), bf16[32,2,4096]{2,1,0:T(2,128)(2,1)S(1)}, u32[]{:S(2)}, u32[]{:S(2)}) async-start(bf16[32,2,4096]{2,1,0:T(2,128)(2,1)} %reshape.310), calls=%async_computation.2 | async-start | bytes 1048576 | tf_op jit(solution)/shard_map/all_to_all | solution.py:121
  225.3 23.2 %copy-start.5 = (bf16[32,2,4096]{2,1,0:T(2,128)(2,1)}, bf16[32,2,4096]{2,1,0:T(2,128)(2,1)S(1)}, u32[]{:S(2)}) copy-start(bf16[32,2,4096]{2,1,0:T(2,128)(2,1)S(1)} %all-to-all-done.1) | copy-start | bytes 1572868
  225.3 23.2 %all-to-all-start.2 = ((bf16[32,2,4096]{2,1,0:T(2,128)(2,1)}), bf16[32,2,4096]{2,1,0:T(2,128)(2,1)S(1)}, u32[]{:S(2)}, u32[]{:S(2)}) async-start(bf16[32,2,4096]{2,1,0:T(2,128)(2,1)} %reshape.312), calls=%async_computation.3 | async-start | bytes 1048576 | tf_op jit(solution)/shard_map/all_to_all | solution.py:122
  248.5 12.8 %copy-start.6 = (bf16[32,2,4096]{2,1,0:T(2,128)(2,1)}, bf16[32,2,4096]{2,1,0:T(2,128)(2,1)S(1)}, u32[]{:S(2)}) copy-start(bf16[32,2,4096]{2,1,0:T(2,128)(2,1)S(1)} %all-to-all-done.2) | copy-start | bytes 1572868
  248.5 26.0 %all-to-all-start.4 = ((bf16[32,2,4096]{2,1,0:T(2,128)(2,1)}), bf16[32,2,4096]{2,1,0:T(2,128)(2,1)S(1)}, u32[]{:S(2)}, u32[]{:S(2)}) async-start(bf16[32,2,4096]{2,1,0:T(2,128)(2,1)} %reshape.316), calls=%async_computation.6 | async-start | bytes 1048576 | tf_op jit(solution)/shard_map/all_to_all | solution.py:123
  274.5 8.6 %copy-start.7 = (bf16[32,2,4096]{2,1,0:T(2,128)(2,1)}, bf16[32,2,4096]{2,1,0:T(2,128)(2,1)S(1)}, u32[]{:S(2)}) copy-start(bf16[32,2,4096]{2,1,0:T(2,128)(2,1)S(1)} %all-to-all-done.4) | copy-start | bytes 1572868
  274.5 26.4 %all-to-all-start.3 = ((bf16[32,2,4096]{2,1,0:T(2,128)(2,1)}), bf16[32,2,4096]{2,1,0:T(2,128)(2,1)}, u32[]{:S(2)}, u32[]{:S(2)}) async-start(bf16[32,2,4096]{2,1,0:T(2,128)(2,1)} %reshape.314), calls=%async_computation.5 | async-start | bytes 1048576 | tf_op jit(solution)/shard_map/all_to_all | solution.py:124
  325.1 7.9 %copy-start.3 = (f32[512,4096]{1,0:T(8,128)S(1)}, f32[512,4096]{1,0:T(8,128)}, u32[]{:S(2)}) copy-start(f32[512,4096]{1,0:T(8,128)} %copy-done.2) | copy-start | bytes 25165828 | tf_op jit(solution)/shard_map/while
  347.9 7.9 %copy-start.3 = (f32[512,4096]{1,0:T(8,128)S(1)}, f32[512,4096]{1,0:T(8,128)}, u32[]{:S(2)}) copy-start(f32[512,4096]{1,0:T(8,128)} %copy-done.2) | copy-start | bytes 25165828 | tf_op jit(solution)/shard_map/while
  370.7 7.9 %copy-start.3 = (f32[512,4096]{1,0:T(8,128)S(1)}, f32[512,4096]{1,0:T(8,128)}, u32[]{:S(2)}) copy-start(f32[512,4096]{1,0:T(8,128)} %copy-done.2) | copy-start | bytes 25165828 | tf_op jit(solution)/shard_map/while
  393.5 7.9 %copy-start.3 = (f32[512,4096]{1,0:T(8,128)S(1)}, f32[512,4096]{1,0:T(8,128)}, u32[]{:S(2)}) copy-start(f32[512,4096]{1,0:T(8,128)} %copy-done.2) | copy-start | bytes 25165828 | tf_op jit(solution)/shard_map/while
  416.2 7.9 %copy-start.3 = (f32[512,4096]{1,0:T(8,128)S(1)}, f32[512,4096]{1,0:T(8,128)}, u32[]{:S(2)}) copy-start(f32[512,4096]{1,0:T(8,128)} %copy-done.2) | copy-start | bytes 25165828 | tf_op jit(solution)/shard_map/while
  522.1 37.6 %all-to-all-start.7 = ((bf16[32,2,4096]{2,1,0:T(2,128)(2,1)}), bf16[32,2,4096]{2,1,0:T(2,128)(2,1)}, u32[]{:S(2)}, u32[]{:S(2)}) async-start(bf16[32,2,4096]{2,1,0:T(2,128)(2,1)} %reshape.322), calls=%async_computation.9 | async-start | bytes 1048576 | tf_op jit(solution)/shard_map/all_to_all | solution.py:130
  559.8 34.7 %all-to-all-start.6 = ((bf16[32,2,4096]{2,1,0:T(2,128)(2,1)}), bf16[32,2,4096]{2,1,0:T(2,128)(2,1)}, u32[]{:S(2)}, u32[]{:S(2)}) async-start(bf16[32,2,4096]{2,1,0:T(2,128)(2,1)} %reshape.320), calls=%async_computation.8 | async-start | bytes 1048576 | tf_op jit(solution)/shard_map/all_to_all | solution.py:129
  594.5 24.1 %all-to-all-start.5 = ((bf16[32,2,4096]{2,1,0:T(2,128)(2,1)}), bf16[32,2,4096]{2,1,0:T(2,128)(2,1)}, u32[]{:S(2)}, u32[]{:S(2)}) async-start(bf16[32,2,4096]{2,1,0:T(2,128)(2,1)} %reshape.318), calls=%async_computation.7 | async-start | bytes 1048576 | tf_op jit(solution)/shard_map/all_to_all | solution.py:128
  618.5 15.1 %copy-start.1 = (bf16[1024,1536]{1,0:T(8,128)(2,1)S(1)}, bf16[1024,1536]{1,0:T(8,128)(2,1)}, u32[]{:S(2)}) copy-start(bf16[1024,1536]{1,0:T(8,128)(2,1)} %param.14) | copy-start | bytes 9437188
  (15 other events, 53.4 us)
Sparse Core Ops, SparseCore 0:
  9.7 31.2 all-gather.2
  51.5 44.2 reduce-scatter.2
  156.9 20.7 all-gather.4
  188.4 64.0 reduce-scatter.4
where the time goes:
time: 653 us; the launch traced here: 640 us
  other arithmetic  205 us (31%)
  matrix products  174 us (27%)
  local copies, waits for them, and re-layouts  114 us (17%)
  waiting for transfers between devices  59.8 us (9%)
  starting transfers between devices  54.5 us (8%)
  blocking collectives  18.1 us (3%)
  between operations  14.4 us (2%)
    unnamed x10, other arithmetic  138 us
    unnamed x57, local copies, waits for them, and re-layouts  67.8 us
    dot_general x8, matrix products, visit(): jnp.einsum('hqk,khd->qhd', grad_s, key_rows, preferred_element_type=jnp.f...  36.5 us
    all_gather x1, waiting for transfers between devices, on_device(): lax.all_gather(hidden, 'dp', axis=0, tiled=True)  33.1 us
    dot_general x8, matrix products, visit(): jnp.einsum('qhd,khd->hqk', grad_blk, value_rows, preferred_element_type=j...  33 us
    reduce_sum x2, other arithmetic, unit_target(): center = jnp.mean(values32, axis=1, keepdims=True)  31.6 us
    dot_general x8, matrix products, visit(): jnp.einsum('hqk,qhd->khd', grad_s, query_blk, preferred_element_type=jnp....  26.6 us
    all_gather x1, waiting for transfers between devices, on_device(): lax.all_gather(grad_z, 'dp', axis=0, tiled=True)  20.6 us
  transfers between devices with their start and end apart: 11, of which 4 were waited for; matrix products, arithmetic and copies ran while one was open for 36% of the time, Pallas kernels for 0%

commit v1 on v0

v1 whole, which is shorter than its diff:
```python
from jax.sharding import PartitionSpec as P
import jax, jax.numpy as jnp
from jax import lax
from jax.experimental import pallas as pl
from jax.experimental.pallas import tpu as pltpu
LOG2E = 1.4426950408889634
F32=jnp.float32; BF=jnp.bfloat16
QB=512; KC=512; L=4096; NB=32; HD=64

def dot(a,b): return jnp.dot(a,b,preferred_element_type=F32)

def kern(q_ref,k_ref,v_ref,g_ref, dq_ref,dk_ref,dv_ref, kk,vv,kt,vt, s_ref,u_ref, ak,av):
    i = pl.program_id(0)
    per = QB//128
    @pl.when(i==0)
    def _():
        for j in range(NB):
            kb=k_ref[j]; vb=v_ref[j]
            rows=pl.ds(j*128,128)
            kn=kb.T; vn=vb.T
            kk[rows,:]=jnp.concatenate([kn,kn],axis=1)
            lane=lax.broadcasted_iota(jnp.int32,(128,HD),1)
            vv[rows,:]=jnp.concatenate([vn,jnp.where(lane<2,1.0,0.0).astype(BF)],axis=1)
            kt[:,rows]=kb*BF(0.125)
            vt[pl.ds(0,HD),rows]=vb
        vt[pl.ds(HD,16),:]=jnp.ones((16,L),BF)
        ak[...]=jnp.zeros_like(ak); av[...]=jnp.zeros_like(av)
    qt=jnp.concatenate([q_ref[i*per+j] for j in range(per)],axis=1)
    gt=jnp.concatenate([g_ref[i*per+j] for j in range(per)],axis=1)
    qf=qt.astype(F32)*(0.125*LOG2E)
    qhi=qf.astype(BF); qlo=(qf-qhi.astype(F32)).astype(BF)
    qa=jnp.concatenate([qhi,qlo],axis=0)
    m=jnp.full((8,QB),-jnp.inf,F32)
    for c in range(L//KC):
        rows=pl.ds(c*KC,KC)
        s=dot(kk[rows,:],qa)
        s_ref[rows,:]=s
        m=jnp.maximum(m,jnp.max(s.reshape(KC//8,8,QB),axis=0))
    m=jnp.max(m,axis=0,keepdims=True)
    acc=jnp.zeros((HD+16,QB),F32)
    for c in range(L//KC):
        rows=pl.ds(c*KC,KC)
        u=jnp.exp2(s_ref[rows,:]-m).astype(BF)
        u_ref[rows,:]=u
        acc=acc+dot(vt[:,rows],u)
    l=acc[HD:HD+1]
    rl=1.0/l
    gf=gt.astype(F32)
    d=-jnp.sum(gf*acc[:HD],axis=0,keepdims=True)*rl
    dhi=d.astype(BF); dlo=(d-dhi.astype(F32))
    row=lax.broadcasted_iota(jnp.int32,(HD,QB),0)
    tail=jnp.where(row==0,dhi.astype(F32),jnp.where(row==1,dlo,0.0)).astype(BF)
    ga=jnp.concatenate([gt,tail],axis=0)
    qn=(qt.astype(F32)*(rl*0.125)).T.astype(BF)
    gn=(gf*rl).T.astype(BF)
    dq=jnp.zeros((HD,QB),F32)
    for c in range(L//KC):
        rows=pl.ds(c*KC,KC)
        u=u_ref[rows,:]
        dp=dot(vv[rows,:],ga)
        ds=(u.astype(F32)*dp).astype(BF)
        ak[rows,:]+=dot(ds,qn)
        av[rows,:]+=dot(u,gn)
        dq=dq+dot(kt[:,rows],ds)
    dq=(dq*rl).astype(BF)
    for j in range(per):
        dq_ref[i*per+j]=dq[:,j*128:(j+1)*128]
    @pl.when(i==pl.num_programs(0)-1)
    def _():
        for j in range(NB):
            rows=pl.ds(j*128,128)
            dk_ref[j]=ak[rows,:].T.astype(BF)
            dv_ref[j]=av[rows,:].T.astype(BF)


def attention(q,k,v,g):
    full=pl.BlockSpec((NB,HD,128),lambda i:(0,0,0))
    return pl.pallas_call(kern,grid=(L//QB,),in_specs=[full]*4,out_specs=[full]*3,
        out_shape=[jax.ShapeDtypeStruct((NB,HD,128),BF)]*3,
        scratch_shapes=[pltpu.VMEM((L,128),BF),pltpu.VMEM((L,128),BF),pltpu.VMEM((HD,L),BF),pltpu.VMEM((HD+16,L),BF),
            pltpu.VMEM((L,QB),F32),pltpu.VMEM((L,QB),BF),pltpu.VMEM((L,HD),F32),pltpu.VMEM((L,HD),F32)],
        compiler_params=pltpu.CompilerParams(vmem_limit_bytes=56*2**20),name="attn")(q,k,v,g)


loss_weight = 1000.0


def unit_target(features):
    values32 = features.astype(jnp.float32)
    center = jnp.mean(values32, axis=1, keepdims=True)
    shifted = values32 - center
    spread = jnp.mean(shifted * shifted, axis=1, keepdims=True)
    normed = shifted * lax.rsqrt(spread + 1e-06)
    unit = normed * lax.rsqrt(jnp.sum(normed * normed, axis=1, keepdims=True) + 1e-06)
    return jnp.transpose(unit, (0, 2, 1))


def cosine_grad(projected, target):
    rinv = lax.rsqrt(jnp.sum(projected * projected, axis=-1, keepdims=True) + 1e-06)
    direction = projected * rinv
    cosine = jnp.sum(direction * target, axis=-1)
    grad_z = -loss_weight * rinv * (target - cosine[..., None] * direction)
    return (cosine, grad_z.astype(jnp.bfloat16))


def silu_slope(pre_act):
    sigma = jax.nn.sigmoid(pre_act)
    return sigma * (1.0 + pre_act * (1.0 - sigma))


def on_device(hidden, out_cot, proj_in, proj_out, attn_out_w, queries, keys, values, dino):
    features = lax.all_to_all(jnp.transpose(dino.reshape(48, 32, 128), (1, 0, 2)), "seq", split_axis=0, concat_axis=0, tiled=True).reshape(1, 1536, 128)
    target = unit_target(features)
    pre_act = jnp.einsum(
        "itd,dh->ith",
        lax.all_gather(hidden, "dp", axis=0, tiled=True),
        proj_in,
        preferred_element_type=jnp.float32,
    )
    silu_out = jax.nn.silu(pre_act).astype(jnp.bfloat16)
    picked = silu_out
    projected = lax.psum_scatter(
        jnp.einsum("ith,hc->itc", picked, proj_out, preferred_element_type=jnp.float32),
        "dp",
        scatter_dimension=0,
        tiled=True,
    )
    cosine, grad_z = cosine_grad(projected, target)
    grad_silu = jnp.einsum(
        "itc,hc->ith",
        lax.all_gather(grad_z, "dp", axis=0, tiled=True),
        proj_out,
        preferred_element_type=jnp.float32,
    )
    grad_pre = (grad_silu * silu_slope(pre_act)).astype(jnp.bfloat16)
    picked = grad_pre
    grad_repa = lax.psum_scatter(
        jnp.einsum("ith,dh->itd", picked, proj_in, preferred_element_type=jnp.float32),
        "dp",
        scatter_dimension=0,
        tiled=True,
    )
    grad_hidden = (out_cot.astype(jnp.float32) + grad_repa).astype(jnp.bfloat16)
    grad_attn = jnp.einsum(
        "itd,ed->ite", grad_hidden, attn_out_w, preferred_element_type=jnp.float32
    ).astype(jnp.bfloat16)
    def to_heads(x):
        blocks = x[0].T.reshape(NB, HD, x.shape[1])
        return lax.all_to_all(blocks, "seq", split_axis=0, concat_axis=0, tiled=True)

    def to_tokens(x):
        blocks = lax.all_to_all(x, "seq", split_axis=0, concat_axis=0, tiled=True)
        return blocks.reshape(NB * HD, x.shape[2]).T[None]

    grad_q, grad_k, grad_v = attention(to_heads(queries), to_heads(keys), to_heads(values), to_heads(grad_attn))
    back_q, back_k, back_v = to_tokens(grad_q), to_tokens(grad_k), to_tokens(grad_v)
    return (cosine, back_q, back_k, back_v)


def solution(mesh):
    in_specs = (
        P("dp", "seq", None),
        P("dp", "seq", None),
        P(None, "dp"),
        P("dp", None),
        P(),
        P("dp", "seq", None),
        P("dp", "seq", None),
        P("dp", "seq", None),
        P("dp", "seq", None),
    )
    out_specs = (P("dp", "seq"), P("dp", "seq", None), P("dp", "seq", None), P("dp", "seq", None))
    return jax.shard_map(
        on_device, mesh=mesh, in_specs=in_specs, out_specs=out_specs, check_vma=False
    )
```

time: 653 us -> 343 us (0.53); the launches traced: 640 us -> 341 us
  other arithmetic: 205 us -> 4.82 us
  matrix products: 174 us -> 28 us
  local copies, waits for them, and re-layouts: 114 us -> 18.1 us
  waiting for transfers between devices: 59.8 us -> 130 us
  Pallas kernels: 0 us -> 58.4 us
  blocking collectives: 18.1 us -> 66.5 us
  starting transfers between devices: 54.5 us -> 21.6 us
    dot_general x48 -> x0, matrix products: 147 us -> none  [the longest x8 36.5 us: visit(): jnp.einsum('hqk,khd->qhd', grad_s, key_rows, preferred_element_type=jnp.f...]
    unnamed x10 -> x0, other arithmetic: 138 us -> none
    unnamed x57 -> x13, local copies, waits for them, and re-layouts: 67.8 us -> 2.36 us
    pallas_call x0 -> x1, Pallas kernels: none -> 58.4 us  [attention(): pl.pallas_call(kern, grid=(L // QB,), in_specs=[full] * 4, out_specs=[ful...]
    all_to_all x1 -> x4, blocking collectives: 18.1 us -> 66.5 us  [the longest x2 29.4 us: to_tokens(): blocks = lax.all_to_all(x, 'seq', split_axis=0, concat_axis=0, tiled=True)]
    all_to_all x7 -> x4, starting transfers between devices: 54.1 us -> 21.4 us  [the longest x3 16.8 us: to_heads(): lax.all_to_all(blocks, 'seq', split_axis=0, concat_axis=0, tiled=True)]
    reduce_sum x2 -> x1, other arithmetic: 31.6 us -> 0.22 us  [unit_target(): center = jnp.mean(values32, axis=1, keepdims=True)]
    all_to_all x7 -> x4, waiting for transfers between devices: 5.38 us -> 29.9 us  [the longest x3 23.9 us: to_heads(): lax.all_to_all(blocks, 'seq', split_axis=0, concat_axis=0, tiled=True)]
  transfers between devices with their start and end apart: 11 -> 8, of which waited for: 4 -> 7; matrix products, arithmetic and copies ran while one was open for 36% -> 7% of each run, Pallas kernels for 0% -> 0%
where the time goes in v1:
time: 343 us; the launch traced here: 341 us
  waiting for transfers between devices  130 us (38%)
  blocking collectives  66.5 us (19%)
  Pallas kernels  58.4 us (17%)
  matrix products  28 us (8%)
  starting transfers between devices  21.6 us (6%)
  local copies, waits for them, and re-layouts  18.1 us (5%)
  between operations  13.9 us (4%)
  other arithmetic  4.82 us (1%)
    pallas_call x1, Pallas kernels, attention(): pl.pallas_call(kern, grid=(L // QB,), in_specs=[full] * 4, out_specs=[ful...  58.4 us
    all_gather x1, waiting for transfers between devices, on_device(): lax.all_gather(hidden, 'dp', axis=0, tiled=True)  33.1 us
    all_to_all x2, blocking collectives, to_tokens(): blocks = lax.all_to_all(x, 'seq', split_axis=0, concat_axis=0, tiled=True)  29.4 us
    all_to_all x3, waiting for transfers between devices, to_heads(): lax.all_to_all(blocks, 'seq', split_axis=0, concat_axis=0, tiled=True)  23.9 us
    reduce_scatter x1, waiting for transfers between devices, on_device(): lax.psum_scatter(jnp.einsum('ith,hc->itc', picked, proj_out, preferred_el...  23.8 us
    all_gather x1, waiting for transfers between devices, on_device(): lax.all_gather(grad_z, 'dp', axis=0, tiled=True)  23.2 us
    reduce_scatter x1, waiting for transfers between devices, on_device(): lax.psum_scatter(jnp.einsum('ith,dh->itd', picked, proj_in, preferred_ele...  19.4 us
    all_to_all x1, blocking collectives, to_heads(): lax.all_to_all(blocks, 'seq', split_axis=0, concat_axis=0, tiled=True)  19.4 us
  transfers between devices with their start and end apart: 8, of which 7 were waited for; matrix products, arithmetic and copies ran while one was open for 7% of the time, Pallas kernels for 0%

profile of v1, /device:TPU:0, one launch (start us, length us, event | category | flops | bytes accessed | tf_op | source)
XLA Modules:
  0.0 341.4 jit_solution(11142184372649594353)
XLA Ops:
  8.0 33.1 %all-gather.3.cloned.1.call-done = bf16[4,128,2432]{2,1,0:T(8,128)(2,1)} async-done(((bf16[1,128,2432]{2,1,0:T(8,128)(2,1)}), bf16[4,128,2432]{2,1,0:T(8,128)(2,1)}) %all-gather.3.cloned.1.call-update) | async-done | bytes 2490384 | tf_op jit(solution)/shard_map/all_gather | solution.py:116
  41.0 5.5 %fusion.2 = f32[4,128,1024]{2,1,0:T(8,128)S(1)} fusion(bf16[4,128,2432]{2,1,0:T(8,128)(2,1)} %all-gather.3.cloned.1.call-done, bf16[2432,1024]{1,0:T(8,128)(2,1)} %param.11), kind=kOutput, calls=%fused_computation.2 | convolution fusion | flops 2550136832 | bytes 9568256 | tf_op jit(solution)/shard_map/itd,dh->ith/dot_general | solution.py:114
  47.9 3.5 %fusion.6 = f32[4,128,1536]{2,1,0:T(8,128)} fusion(bf16[1024,1536]{1,0:T(8,128)(2,1)S(1)} %copy-done, f32[4,128,1024]{2,1,0:T(8,128)S(1)} %fusion.2), kind=kOutput, calls=%fused_computation.6 | convolution fusion | flops 1613234176 | bytes 8388608 | tf_op jit(solution)/shard_map/ith,hc->itc/dot_general | solution.py:123
  52.6 17.7 %all_to_all.40 = bf16[32,48,128]{2,1,0:T(8,128)(2,1)S(1)} all-to-all(bf16[32,48,128]{2,1,0:T(8,128)(2,1)S(1)} %copy.38), channel_id=1, replica_groups=mesh['dp'=4,'seq'=32] {'seq'}, dimensions={0} | all-to-all | bytes 786432 | tf_op jit(solution)/shard_map/all_to_all | solution.py:112
  72.1 23.8 %reduce-scatter.3.cloned.1.call-done = f32[1,128,1536]{2,1,0:T(8,128)} async-done(((f32[4,128,1536]{2,1,0:T(8,128)}), f32[1,128,1536]{2,1,0:T(8,128)}) %reduce-scatter.3.cloned.1.call-update) | async-done | bytes 786448 | tf_op jit(solution)/shard_map/reduce_scatter | solution.py:122
  100.1 23.2 %all-gather.5.cloned.1.call-done = bf16[4,128,1536]{2,1,0:T(8,128)(2,1)} async-done(((bf16[1,128,1536]{2,1,0:T(8,128)(2,1)}), bf16[4,128,1536]{2,1,0:T(8,128)(2,1)}) %all-gather.5.cloned.1.call-update) | async-done | bytes 1572880 | tf_op jit(solution)/shard_map/all_gather | solution.py:131
  123.4 10.5 %fusion = f32[4,128,2432]{2,1,0:T(8,128)} fusion(bf16[2432,1024]{1,0:T(8,128)(2,1)} %param.11, f32[4,128,1024]{2,1,0:T(8,128)} %copy-done.5, bf16[4,128,1536]{2,1,0:T(8,128)(2,1)} %all-gather.5.cloned.1.call-done, bf16[1024,1536]{1,0:T(8,128)(2,1)S(1)} %copy-done), kind=kOutput, calls=%fused_computation | convolution fusion | flops 4165468160 | bytes 16777216 | tf_op jit(solution)/shard_map/ith,dh->itd/dot_general | solution.py:138
  133.9 2.0 copy.40
  136.0 7.4 %all-to-all-start.1 = ((bf16[32,64,128]{2,1,0:T(8,128)(2,1)}), bf16[32,64,128]{2,1,0:T(8,128)(2,1)}, u32[]{:S(2)}, u32[]{:S(2)}) async-start(bf16[32,64,128]{2,1,0:T(8,128)(2,1)} %bitcast.70), calls=%async_computation.2 | async-start | bytes 1048576 | tf_op jit(solution)/shard_map/all_to_all | solution.py:149
  143.4 2.2 copy.41
  145.6 9.7 %all-to-all-done.1.q_ref = bf16[32,64,128]{2,1,0:T(8,128)(2,1)} async-done(((bf16[32,64,128]{2,1,0:T(8,128)(2,1)}), bf16[32,64,128]{2,1,0:T(8,128)(2,1)}, u32[]{:S(2)}, u32[]{:S(2)}) %all-to-all-start.1) | async-done | bytes 524320 | tf_op jit(solution)/shard_map/all_to_all | solution.py:149
  155.2 4.6 %all-to-all-start.2 = ((bf16[32,64,128]{2,1,0:T(8,128)(2,1)}), bf16[32,64,128]{2,1,0:T(8,128)(2,1)}, u32[]{:S(2)}, u32[]{:S(2)}) async-start(bf16[32,64,128]{2,1,0:T(8,128)(2,1)} %bitcast.66), calls=%async_computation.3 | async-start | bytes 1048576 | tf_op jit(solution)/shard_map/all_to_all | solution.py:149
  159.9 2.0 copy.42
  161.9 14.2 %all-to-all-done.2.k_ref = bf16[32,64,128]{2,1,0:T(8,128)(2,1)} async-done(((bf16[32,64,128]{2,1,0:T(8,128)(2,1)}), bf16[32,64,128]{2,1,0:T(8,128)(2,1)}, u32[]{:S(2)}, u32[]{:S(2)}) %all-to-all-start.2) | async-done | bytes 524320 | tf_op jit(solution)/shard_map/all_to_all | solution.py:149
  176.1 4.8 %all-to-all-start.3 = ((bf16[32,64,128]{2,1,0:T(8,128)(2,1)}), bf16[32,64,128]{2,1,0:T(8,128)(2,1)}, u32[]{:S(2)}, u32[]{:S(2)}) async-start(bf16[32,64,128]{2,1,0:T(8,128)(2,1)} %bitcast.65), calls=%async_computation.4 | async-start | bytes 1048576 | tf_op jit(solution)/shard_map/all_to_all | solution.py:149
  180.9 19.4 %reduce-scatter.5.cloned.1.call-done = f32[1,128,2432]{2,1,0:T(8,128)} async-done(((f32[4,128,2432]{2,1,0:T(8,128)}), f32[1,128,2432]{2,1,0:T(8,128)}) %reduce-scatter.5.cloned.1.call-update) | async-done | bytes 1245200 | tf_op jit(solution)/shard_map/reduce_scatter | solution.py:137
  200.3 8.5 %fusion.8 = bf16[2048,128]{0,1:T(8,128)(2,1)} fusion(bf16[2048,2432]{1,0:T(8,128)(2,1)} %param.13, f32[1,128,2432]{2,1,0:T(8,128)} %reduce-scatter.5.cloned.1.call-done, bf16[1,128,2432]{2,1,0:T(8,128)(2,1)} %param.10), kind=kOutput, calls=%fused_computation.9 | convolution fusion | flops 1276264448 | bytes 12353536 | tf_op jit(solution)/shard_map/itd,ed->ite/dot_general | solution.py:144
  210.9 19.4 %all_to_all.41.g_ref = bf16[32,64,128]{2,1,0:T(8,128)(2,1)} all-to-all(bf16[32,64,128]{2,1,0:T(8,128)(2,1)} %bitcast.69), channel_id=1, replica_groups=mesh['dp'=4,'seq'=32] {'seq'}, dimensions={0} | all-to-all | bytes 1048576 | tf_op jit(solution)/shard_map/all_to_all | solution.py:149
  230.3 58.4 %attn.1 = (bf16[32,64,128]{2,1,0:T(8,128)(2,1)}, bf16[32,64,128]{2,1,0:T(8,128)(2,1)}, bf16[32,64,128]{2,1,0:T(8,128)(2,1)}) custom-call(bf16[32,64,128]{2,1,0:T(8,128)(2,1)} %all-to-all-done.1.q_ref, bf16[32,64,128]{2,1,0:T(8,128)(2,1)} %all-to-all-done.2.k_ref, bf16[32,64,128]{2,1,0:T(8,128)(2,1)} %all-to-all-done.3.v_ref, ...), custom_call_target="tpu_custom_call" | custom-call | tf_op jit(solution)/shard_map/attn/pallas_call | solution.py:78
  288.7 14.7 %all_to_all.42 = bf16[32,64,128]{2,1,0:T(8,128)(2,1)} all-to-all(bf16[32,64,128]{2,1,0:T(8,128)(2,1)} %get-tuple-element.7), channel_id=1, replica_groups=mesh['dp'=4,'seq'=32] {'seq'}, dimensions={0} | all-to-all | bytes 1048576 | tf_op jit(solution)/shard_map/all_to_all | solution.py:152
  303.4 14.7 %all_to_all.43 = bf16[32,64,128]{2,1,0:T(8,128)(2,1)} all-to-all(bf16[32,64,128]{2,1,0:T(8,128)(2,1)} %get-tuple-element.8), channel_id=1, replica_groups=mesh['dp'=4,'seq'=32] {'seq'}, dimensions={0} | all-to-all | bytes 1048576 | tf_op jit(solution)/shard_map/all_to_all | solution.py:152
  318.1 4.6 %all-to-all-start.7 = ((bf16[32,64,128]{2,1,0:T(8,128)(2,1)}), bf16[32,64,128]{2,1,0:T(8,128)(2,1)}, u32[]{:S(2)}, u32[]{:S(2)}) async-start(bf16[32,64,128]{2,1,0:T(8,128)(2,1)} %get-tuple-element.9), calls=%async_computation.9 | async-start | bytes 1048576 | tf_op jit(solution)/shard_map/all_to_all | solution.py:152
  322.7 2.0 copy.44
  326.8 6.0 %all-to-all-done.7 = bf16[32,64,128]{2,1,0:T(8,128)(2,1)} async-done(((bf16[32,64,128]{2,1,0:T(8,128)(2,1)}), bf16[32,64,128]{2,1,0:T(8,128)(2,1)}, u32[]{:S(2)}, u32[]{:S(2)}) %all-to-all-start.7) | async-done | bytes 524320 | tf_op jit(solution)/shard_map/all_to_all | solution.py:152
  (37 shorter events, 15.4 us)
Async XLA Ops:
  7.2 40.7 %copy-start = (bf16[1024,1536]{1,0:T(8,128)(2,1)S(1)}, bf16[1024,1536]{1,0:T(8,128)(2,1)}, u32[]{:S(2)}) copy-start(bf16[1024,1536]{1,0:T(8,128)(2,1)} %param.12) | copy-start | bytes 9437188
  7.2 33.8 %all-gather.3.cloned.1.call-start = ((), (), s32[]{:S(2)}) async-start(), calls=%async_computation.10 | async-start | bytes 3112960 | tf_op jit(solution)/shard_map/all_gather | solution.py:116
  7.9 88.0 %reduce-scatter.3.cloned.1.call-start = ((), (), s32[]{:S(2)}) async-start(), calls=%async_computation.11 | async-start | bytes 3932160 | tf_op jit(solution)/shard_map/reduce_scatter | solution.py:122
  46.5 1.4 copy-start.5
  51.4 1.0 copy-start.3
  51.4 72.0 %all-gather.5.cloned.1.call-start = ((), (), s32[]{:S(2)}) async-start(), calls=%async_computation.12 | async-start | bytes 1966080 | tf_op jit(solution)/shard_map/all_gather | solution.py:131
  95.9 3.1 copy-start.1
  95.9 3.1 copy-start.2
  98.9 34.9 %copy-start.4 = (f32[128]{0:T(128)}, f32[128]{0:T(128)S(1)}, u32[]{:S(2)}) copy-start(f32[128]{0:T(128)S(1)} %fusion.14) | copy-start | bytes 1540
  100.1 100.3 %reduce-scatter.5.cloned.1.call-start = ((), (), s32[]{:S(2)}) async-start(), calls=%async_computation.13 | async-start | bytes 6225920 | tf_op jit(solution)/shard_map/reduce_scatter | solution.py:137
  136.0 19.3 %all-to-all-start.1 = ((bf16[32,64,128]{2,1,0:T(8,128)(2,1)}), bf16[32,64,128]{2,1,0:T(8,128)(2,1)}, u32[]{:S(2)}, u32[]{:S(2)}) async-start(bf16[32,64,128]{2,1,0:T(8,128)(2,1)} %bitcast.70), calls=%async_computation.2 | async-start | bytes 1048576 | tf_op jit(solution)/shard_map/all_to_all | solution.py:149
  155.2 20.9 %all-to-all-start.2 = ((bf16[32,64,128]{2,1,0:T(8,128)(2,1)}), bf16[32,64,128]{2,1,0:T(8,128)(2,1)}, u32[]{:S(2)}, u32[]{:S(2)}) async-start(bf16[32,64,128]{2,1,0:T(8,128)(2,1)} %bitcast.66), calls=%async_computation.3 | async-start | bytes 1048576 | tf_op jit(solution)/shard_map/all_to_all | solution.py:149
  176.1 34.7 %all-to-all-start.3 = ((bf16[32,64,128]{2,1,0:T(8,128)(2,1)}), bf16[32,64,128]{2,1,0:T(8,128)(2,1)}, u32[]{:S(2)}, u32[]{:S(2)}) async-start(bf16[32,64,128]{2,1,0:T(8,128)(2,1)} %bitcast.65), calls=%async_computation.4 | async-start | bytes 1048576 | tf_op jit(solution)/shard_map/all_to_all | solution.py:149
  318.1 14.7 %all-to-all-start.7 = ((bf16[32,64,128]{2,1,0:T(8,128)(2,1)}), bf16[32,64,128]{2,1,0:T(8,128)(2,1)}, u32[]{:S(2)}, u32[]{:S(2)}) async-start(bf16[32,64,128]{2,1,0:T(8,128)(2,1)} %get-tuple-element.9), calls=%async_computation.9 | async-start | bytes 1048576 | tf_op jit(solution)/shard_map/all_to_all | solution.py:152
Sparse Core Ops, SparseCore 0:
  9.7 31.2 all-gather.2
  51.5 44.3 reduce-scatter.2
  100.2 23.1 all-gather.4
  134.0 66.2 reduce-scatter.4

commit v2 on v1

v2 whole, which is shorter than its diff:
```python
import jax
import jax.numpy as jnp
from jax import lax
from jax.experimental import pallas as pl
from jax.experimental.pallas import tpu as pltpu
from jax.sharding import PartitionSpec as P

LOG2E = 1.4426950408889634
F32=jnp.float32; BF=jnp.bfloat16
QB=512; KC=512; L=4096; NB=32; HD=64
T=128; D=2432; HID=1024; C=1536
MESH=pl.DeviceIdType.MESH
LOSS_WEIGHT=1000.0

def dot(a,b): return jnp.dot(a,b,preferred_element_type=F32)
def dot_nt(a,b): return lax.dot_general(a,b,(((1,),(1,)),((),())),preferred_element_type=F32)

def attn_kernel(x_ref,g_ref,o_ref, kk,vv,kt,vt, s_ref,u_ref, ak,av):
    i = pl.program_id(0)
    per = QB//128
    @pl.when(i==0)
    def _():
        for j in range(NB):
            kb=x_ref[j,HD:2*HD]; vb=x_ref[j,2*HD:]
            rows=pl.ds(j*128,128)
            kn=kb.T; vn=vb.T
            kk[rows,:]=jnp.concatenate([kn,kn],axis=1)
            lane=lax.broadcasted_iota(jnp.int32,(128,HD),1)
            vv[rows,:]=jnp.concatenate([vn,jnp.where(lane<2,1.0,0.0).astype(BF)],axis=1)
            kt[:,rows]=kb*BF(0.125)
            vt[pl.ds(0,HD),rows]=vb
        vt[pl.ds(HD,16),:]=jnp.ones((16,L),BF)
        ak[...]=jnp.zeros_like(ak); av[...]=jnp.zeros_like(av)
    qt=jnp.concatenate([x_ref[i*per+j,:HD] for j in range(per)],axis=1)
    gt=jnp.concatenate([g_ref[i*per+j] for j in range(per)],axis=1)
    qf=qt.astype(F32)*(0.125*LOG2E)
    qhi=qf.astype(BF); qlo=(qf-qhi.astype(F32)).astype(BF)
    qa=jnp.concatenate([qhi,qlo],axis=0)
    m=jnp.full((8,QB),-jnp.inf,F32)
    for c in range(L//KC):
        rows=pl.ds(c*KC,KC)
        s=dot(kk[rows,:],qa)
        s_ref[rows,:]=s
        m=jnp.maximum(m,jnp.max(s.reshape(KC//8,8,QB),axis=0))
    m=jnp.max(m,axis=0,keepdims=True)
    acc=jnp.zeros((HD+16,QB),F32)
    for c in range(L//KC):
        rows=pl.ds(c*KC,KC)
        u=jnp.exp2(s_ref[rows,:]-m).astype(BF)
        u_ref[rows,:]=u
        acc=acc+dot(vt[:,rows],u)
    l=acc[HD:HD+1]
    rl=1.0/l
    gf=gt.astype(F32)
    d=-jnp.sum(gf*acc[:HD],axis=0,keepdims=True)*rl
    dhi=d.astype(BF); dlo=(d-dhi.astype(F32))
    row=lax.broadcasted_iota(jnp.int32,(HD,QB),0)
    tail=jnp.where(row==0,dhi.astype(F32),jnp.where(row==1,dlo,0.0)).astype(BF)
    ga=jnp.concatenate([gt,tail],axis=0)
    qn=(qt.astype(F32)*(rl*0.125)).T.astype(BF)
    gn=(gf*rl).T.astype(BF)
    dq=jnp.zeros((HD,QB),F32)
    for c in range(L//KC):
        rows=pl.ds(c*KC,KC)
        u=u_ref[rows,:]
        dp=dot(vv[rows,:],ga)
        ds=(u.astype(F32)*dp).astype(BF)
        ak[rows,:]+=dot(ds,qn)
        av[rows,:]+=dot(u,gn)
        dq=dq+dot(kt[:,rows],ds)
    dq=(dq*rl).astype(BF)
    for j in range(per):
        o_ref[i*per+j,:HD]=dq[:,j*128:(j+1)*128]
    @pl.when(i==pl.num_programs(0)-1)
    def _():
        for j in range(NB):
            rows=pl.ds(j*128,128)
            o_ref[j,HD:2*HD]=ak[rows,:].T.astype(BF)
            o_ref[j,2*HD:]=av[rows,:].T.astype(BF)


def attention(x,g):
    xs=pl.BlockSpec((NB,3*HD,128),lambda i:(0,0,0))
    gs=pl.BlockSpec((NB,HD,128),lambda i:(0,0,0))
    return pl.pallas_call(attn_kernel,grid=(L//QB,),in_specs=[xs,gs],out_specs=xs,
        out_shape=jax.ShapeDtypeStruct((NB,3*HD,128),BF),
        scratch_shapes=[pltpu.VMEM((L,128),BF),pltpu.VMEM((L,128),BF),pltpu.VMEM((HD,L),BF),pltpu.VMEM((HD+16,L),BF),
            pltpu.VMEM((L,QB),F32),pltpu.VMEM((L,QB),BF),pltpu.VMEM((L,HD),F32),pltpu.VMEM((L,HD),F32)],
        compiler_params=pltpu.CompilerParams(vmem_limit_bytes=56*2**20),name="attention")(x,g)


def remote(src,dst,send,recv,dev):
    return pltpu.make_async_remote_copy(src_ref=src,dst_ref=dst,send_sem=send,recv_sem=recv,device_id=dev,device_id_type=MESH)


def wait_bytes(ref,sem):
    pltpu.make_async_copy(ref,ref,sem).wait()


def greet(devs_seq,dp,seq,extra):
    barrier=pltpu.get_barrier_semaphore()
    def hello(r,c):
        pl.semaphore_signal(barrier,inc=1,device_id=(dp,lax.rem(seq+r,NB)),device_id_type=MESH)
        return c
    lax.fori_loop(1,NB,hello,0)
    for dev in extra:
        pl.semaphore_signal(barrier,inc=1,device_id=dev,device_id_type=MESH)
    pl.semaphore_wait(barrier,NB-1+len(extra))


def front_kernel(hid,cot,q,k,v,wi_h,wo_h,wa_h,dino, cos_o,x_o,g_o,
        wi,wo,wa,xt,gt,feat,X,Z,pre,sil,p1s,p1c,p1p,p1r,p1q,p2s,p2c,p2p,p2r,p2q,
        wsem,xsem,fsem,gsem,hs,hr,zs,zr,s1,r1,s2,r2):
    dp=lax.axis_index("dp"); seq=lax.axis_index("seq")
    core=lax.rem(dp,2); hi=dp//2
    partner=(hi*2+(1-core),seq)
    cross_seq=lax.rem(seq+NB//2,NB)
    cross=((1-hi)*2+core,cross_seq)
    diag=((1-hi)*2+(1-core),cross_seq)
    loads=[pltpu.make_async_copy(a,b,wsem.at[n]) for n,(a,b) in enumerate(((wi_h,wi),(wo_h,wo),(wa_h,wa)))]
    for ld in loads: ld.start()
    greet(None,dp,seq,(partner,cross))
    H=T//2
    def half(ref,h): return ref.at[pl.ds(h*H,H)]
    hc=[remote(half(hid,h),X.at[2,pl.ds(h*H,H)],hs.at[h],hr.at[h],cross) for h in range(2)]
    hp=remote(hid,X.at[1],hs.at[2],hr.at[2],partner)
    hf=[remote(X.at[2,pl.ds(h*H,H)],X.at[3,pl.ds(h*H,H)],hs.at[3+h],hr.at[3+h],partner) for h in range(2)]
    for c in hc: c.start()
    hp.start()
    def send_feat(r,c):
        peer=lax.rem(seq+r,NB)
        remote(dino.at[:,pl.ds(pl.multiple_of(peer*T,T),T)],feat.at[seq],fsem.at[0],fsem.at[1],(dp,peer)).start()
        return c
    pltpu.make_async_copy(dino.at[:,pl.ds(pl.multiple_of(seq*T,T),T)],feat.at[seq],fsem.at[1]).start()
    def turn(p):
        cols=pl.ds(pl.multiple_of(p*T,T),T)
        for n,ref in enumerate((q,k,v)):
            t=ref[:,cols].T
            xt[2*p,pl.ds(n*HD,HD)]=t[:HD]
            xt[2*p+1,pl.ds(n*HD,HD)]=t[HD:]
    base=seq//2
    turn(base)
    pltpu.make_async_copy(xt.at[seq],x_o.at[seq],xsem.at[1]).start()
    mate=base*2+(1-lax.rem(seq,2))
    remote(xt.at[mate],x_o.at[seq],xsem.at[0],xsem.at[1],(dp,mate)).start()
    def turn_send(i,c):
        p=lax.rem(base+i,NB//2)
        turn(p)
        for e in range(2):
            remote(xt.at[2*p+e],x_o.at[seq],xsem.at[0],xsem.at[1],(dp,2*p+e)).start()
        return c
    lax.fori_loop(1,NB//2,turn_send,0)
    lax.fori_loop(1,NB,send_feat,0)
    X[0]=hid[...]
    loads[0].wait()
    hp.wait_recv()
    def first(at,rows):
        def body(n,c):
            cols=pl.ds(pl.multiple_of(n*256,256),256)
            y=dot(X[at:at+2].reshape(2*T,D),wi[:,cols])
            pre[pl.ds(rows,2*T),cols]=y
            sil[pl.ds(rows,2*T),cols]=(y/(1.0+jnp.exp(-y))).astype(BF)
            return c
        lax.fori_loop(0,HID//256,body,0)
    first(0,0)
    for h in range(2):
        hc[h].wait_recv(); hf[h].start()
    for h in range(2): hf[h].wait_recv()
    first(2,2*T)
    loads[1].wait()
    def second(n,c):
        cols=pl.ds(pl.multiple_of(n*256,256),256)
        y=dot(sil[2*T:],wo[:,cols])
        p1c[:,cols]=y[:T]
        p1s[0,:,cols]=y[T:].astype(BF)
        return c
    lax.fori_loop(0,C//256,second,0)
    c1=remote(p1s.at[0],p1r.at[0],s1.at[0],r1.at[0],partner); c1.start()
    def second_own(n,c):
        cols=pl.ds(pl.multiple_of(n*256,256),256)
        y=dot(sil[:2*T],wo[:,cols])
        p1q[:,cols]=y[:T]
        p1s[1,:,cols]=y[T:].astype(BF)
        return c
    lax.fori_loop(0,C//256,second_own,0)
    c2=remote(p1s.at[1],p1r.at[1],s1.at[1],r1.at[1],partner); c2.start()
    c1.wait_recv()
    p1p[...]=(p1c[...]+p1r[0].astype(F32)).astype(BF)
    c3=remote(p1p,p1r.at[2],s1.at[2],r1.at[2],cross); c3.start()
    wait_bytes(feat,fsem.at[1])
    f=feat[...].astype(F32)
    mean=jnp.sum(jnp.sum(f,axis=0),axis=0,keepdims=True)*(1.0/C)
    sh=f-mean[None]
    var=jnp.sum(jnp.sum(sh*sh,axis=0),axis=0,keepdims=True)*(1.0/C)
    sh=sh*lax.rsqrt(var+1e-6)[None]
    nn=jnp.sum(jnp.sum(sh*sh,axis=0),axis=0,keepdims=True)
    sh=sh*lax.rsqrt(nn+1e-6)[None]
    target=sh.reshape(C,T).T
    c2.wait_recv(); c3.wait_recv()
    pr=p1q[...]+p1r[1].astype(F32)+p1r[2].astype(F32)
    rinv=lax.rsqrt(jnp.sum(pr*pr,axis=1,keepdims=True)+1e-6)
    direction=pr*rinv
    cosine=jnp.sum(direction*target,axis=1,keepdims=True)
    ii=lax.broadcasted_iota(jnp.int32,(T,T),0); jj=lax.broadcasted_iota(jnp.int32,(T,T),1)
    cos_o[...]=jnp.sum(jnp.where(ii==jj,cosine,0.0),axis=0,keepdims=True)
    Z[0]=(-LOSS_WEIGHT*rinv*(target-cosine*direction)).astype(BF)
    zc=[remote(Z.at[0,pl.ds(h*H,H)],Z.at[2,pl.ds(h*H,H)],zs.at[h],zr.at[h],cross) for h in range(2)]
    zp=remote(Z.at[0],Z.at[1],zs.at[2],zr.at[2],partner)
    zf=[remote(Z.at[2,pl.ds(h*H,H)],Z.at[3,pl.ds(h*H,H)],zs.at[3+h],zr.at[3+h],partner) for h in range(2)]
    for c in zc: c.start()
    zp.start()
    zp.wait_recv()
    def back(at,rows):
        def body(n,c):
            cols=pl.ds(pl.multiple_of(n*256,256),256)
            gs=dot_nt(Z[at:at+2].reshape(2*T,C),wo[cols,:])
            y=pre[pl.ds(rows,2*T),cols]
            s=1.0/(1.0+jnp.exp(-y))
            sil[pl.ds(rows,2*T),cols]=(gs*(s*(1.0+y*(1.0-s)))).astype(BF)
            return c
        lax.fori_loop(0,HID//256,body,0)
    back(0,0)
    for h in range(2):
        zc[h].wait_recv(); zf[h].start()
    for h in range(2): zf[h].wait_recv()
    back(2,2*T)
    def third(n,c):
        cols=pl.ds(pl.multiple_of(n*128,128),128)
        y=dot_nt(sil[2*T:],wi[cols,:])
        p2c[:,cols]=y[:T]
        p2s[0,:,cols]=y[T:].astype(BF)
        return c
    lax.fori_loop(0,D//128,third,0)
    d1=remote(p2s.at[0],p2r.at[0],s2.at[0],r2.at[0],partner); d1.start()
    def third_own(n,c):
        cols=pl.ds(pl.multiple_of(n*128,128),128)
        y=dot_nt(sil[:2*T],wi[cols,:])
        p2q[:,cols]=y[:T]
        p2s[1,:,cols]=y[T:].astype(BF)
        return c
    d1.wait_recv()
    p2p[...]=(p2c[...]+p2r[0].astype(F32)).astype(BF)
    d3=remote(p2p,p2r.at[2],s2.at[2],r2.at[2],cross); d3.start()
    lax.fori_loop(0,D//128,third_own,0)
    d2=remote(p2s.at[1],p2r.at[1],s2.at[1],r2.at[1],partner); d2.start()
    loads[2].wait()
    d2.wait_recv(); d3.wait_recv()
    gh=(cot[...].astype(F32)+(p2q[...]+p2r[1].astype(F32)+p2r[2].astype(F32))).astype(BF)
    R=512
    def heads(i,c):
        at=lax.rem(seq//8+i,L//2//R)
        y=dot_nt(wa[pl.ds(pl.multiple_of(at*R,R),R)],Z2[...]).astype(BF)
        gt[pl.ds(at*8,8)]=y.reshape(8,HD,T)
        for e in range(8):
            h=at*8+lax.rem(seq+e,8)
            @pl.when(h!=seq)
            def _():
                remote(gt.at[h],g_o.at[seq],gsem.at[0],gsem.at[1],(dp,h)).start()
            @pl.when(h==seq)
            def _():
                pltpu.make_async_copy(gt.at[h],g_o.at[seq],gsem.at[1]).start()
        return c
    Z2=X.at[0]
    X[0]=gh
    lax.fori_loop(0,4,heads,0)
    for c in hc+[hp]+hf+zc+[zp]+zf+[c1,c2,c3,d1,d2,d3]: c.wait_send()
    wait_bytes(x_o,xsem.at[1]); wait_bytes(xt.at[pl.ds(0,NB-1)],xsem.at[0])
    wait_bytes(feat.at[pl.ds(0,NB-1)],fsem.at[0])
    wait_bytes(g_o,gsem.at[1]); wait_bytes(gt.at[pl.ds(0,NB-1)],gsem.at[0])


def front(hid,cot,q,k,v,wi,wo,wa,dino):
    vm=pl.BlockSpec(memory_space=pltpu.VMEM); hb=pl.BlockSpec(memory_space=pl.ANY)
    V=pltpu.VMEM; S=pltpu.SemaphoreType.DMA
    return pl.pallas_call(front_kernel,
        in_specs=[vm]*5+[hb]*3+[vm],out_specs=[vm,hb,hb],
        out_shape=[jax.ShapeDtypeStruct((1,T),F32),jax.ShapeDtypeStruct((NB,3*HD,T),BF),jax.ShapeDtypeStruct((NB,HD,T),BF)],
        scratch_shapes=[V((D,HID),BF),V((HID,C),BF),V((2048,D),BF),V((NB,3*HD,T),BF),V((NB,HD,T),BF),V((NB,48,T),BF),
            V((4,T,D),BF),V((4,T,C),BF),V((4*T,HID),F32),V((4*T,HID),BF),
            V((2,T,C),BF),V((T,C),F32),V((T,C),BF),V((3,T,C),BF),V((T,C),F32),
            V((2,T,D),BF),V((T,D),F32),V((T,D),BF),V((3,T,D),BF),V((T,D),F32),
            S((3,)),S((2,)),S((2,)),S((2,)),S((5,)),S((5,)),S((5,)),S((5,)),S((3,)),S((3,)),S((3,)),S((3,))],
        compiler_params=pltpu.CompilerParams(collective_id=0,has_side_effects=True,vmem_limit_bytes=56*2**20),
        name="front")(hid,cot,q,k,v,wi,wo,wa,dino)


def back_kernel(o_ref,q_o,k_o,v_o,buf,sem):
    dp=lax.axis_index("dp"); seq=lax.axis_index("seq")
    greet(None,dp,seq,())
    pltpu.make_async_copy(o_ref.at[seq],buf.at[seq],sem.at[1]).start()
    def send(r,c):
        peer=lax.rem(seq+r,NB)
        remote(o_ref.at[peer],buf.at[seq],sem.at[0],sem.at[1],(dp,peer)).start()
        return c
    lax.fori_loop(1,NB,send,0)
    wait_bytes(buf,sem.at[1])
    for n,ref in enumerate((q_o,k_o,v_o)):
        for p in range(NB//2):
            ref[:,p*T:(p+1)*T]=buf[2*p:2*p+2,n*HD:(n+1)*HD].reshape(T,T).T
    wait_bytes(buf.at[pl.ds(0,NB-1)],sem.at[0])


def back(o):
    vm=pl.BlockSpec(memory_space=pltpu.VMEM)
    return pl.pallas_call(back_kernel,in_specs=[vm],out_specs=[vm]*3,
        out_shape=[jax.ShapeDtypeStruct((T,NB*HD),BF)]*3,
        scratch_shapes=[pltpu.VMEM((NB,3*HD,T),BF),pltpu.SemaphoreType.DMA((2,))],
        compiler_params=pltpu.CompilerParams(collective_id=1,has_side_effects=True,vmem_limit_bytes=32*2**20),
        name="back")(o)


def on_device(hidden,out_cot,proj_in,proj_out,attn_out_w,queries,keys,values,dino):
    cosine,x,g=front(hidden[0],out_cot[0],queries[0],keys[0],values[0],proj_in,proj_out,attn_out_w,dino[0])
    gq,gk,gv=back(attention(x,g))
    return cosine,gq[None],gk[None],gv[None]


def solution(mesh):
    in_specs = (
        P("dp", "seq", None),
        P("dp", "seq", None),
        P(None, "dp"),
        P("dp", None),
        P(),
        P("dp", "seq", None),
        P("dp", "seq", None),
        P("dp", "seq", None),
        P("dp", "seq", None),
    )
    out_specs = (P("dp", "seq"), P("dp", "seq", None), P("dp", "seq", None), P("dp", "seq", None))
    return jax.shard_map(
        on_device, mesh=mesh, in_specs=in_specs, out_specs=out_specs, check_vma=False
    )
```

time: 343 us -> 179 us (0.52)
  waiting for transfers between devices: 130 us -> 0 us
  Pallas kernels: 58.4 us -> 174 us
  blocking collectives: 66.5 us -> 0 us
  matrix products: 28 us -> 0 us
  starting transfers between devices: 21.6 us -> 0 us
  local copies, waits for them, and re-layouts: 18.1 us -> 4.3 us
  between operations: 13.9 us -> 0.67 us
  other arithmetic: 4.82 us -> 0 us
    pallas_call x1 -> x3, Pallas kernels: 58.4 us -> 174 us  [the longest x1 89.8 us: front(): pl.pallas_call(front_kernel, in_specs=[vm] * 5 + [hb] * 3 + [vm], out_spe...]
    all_to_all x4 -> x0, blocking collectives: 66.5 us -> none  [the longest x2 29.4 us: to_tokens(): blocks = lax.all_to_all(x, 'seq', split_axis=0, concat_axis=0, tiled=True)]
    all_gather x2 -> x0, waiting for transfers between devices: 56.3 us -> none  [the longest x1 33.1 us: on_device(): lax.all_gather(hidden, 'dp', axis=0, tiled=True)]
    reduce_scatter x2 -> x0, waiting for transfers between devices: 43.2 us -> none  [the longest x1 23.8 us: on_device(): lax.psum_scatter(jnp.einsum('ith,hc->itc', picked, proj_out, preferred_el...]
    all_to_all x4 -> x0, waiting for transfers between devices: 29.9 us -> none  [the longest x3 23.9 us: to_heads(): lax.all_to_all(blocks, 'seq', split_axis=0, concat_axis=0, tiled=True)]
    dot_general x4 -> x0, matrix products: 28 us -> none  [the longest x1 10.5 us: on_device(): jnp.einsum('ith,dh->itd', picked, proj_in, preferred_element_type=jnp.flo...]
    all_to_all x4 -> x0, starting transfers between devices: 21.4 us -> none  [the longest x3 16.8 us: to_heads(): lax.all_to_all(blocks, 'seq', split_axis=0, concat_axis=0, tiled=True)]
    transpose x4 -> x0, local copies, waits for them, and re-layouts: 6.46 us -> none  [the longest x3 6.3 us: to_heads(): blocks = x[0].T.reshape(NB, HD, x.shape[1])]
  transfers between devices with their start and end apart: 8 -> 0, of which waited for: 7 -> 0; matrix products, arithmetic and copies ran while one was open for 7% -> 0% of each run, Pallas kernels for 0% -> 0%
where the time goes in v2:
time: 179 us
  Pallas kernels  174 us (97%)
  local copies, waits for them, and re-layouts  4.3 us (2%)
    pallas_call x1, Pallas kernels, front(): pl.pallas_call(front_kernel, in_specs=[vm] * 5 + [hb] * 3 + [vm], out_spe...  89.8 us
    pallas_call x1, Pallas kernels, attention(): pl.pallas_call(attn_kernel, grid=(L // QB,), in_specs=[xs, gs], out_specs...  58.4 us
    pallas_call x1, Pallas kernels, back(): pl.pallas_call(back_kernel, in_specs=[vm], out_specs=[vm] * 3, out_shape=...  25.8 us
    unnamed x8, local copies, waits for them, and re-layouts  4.3 us

profile of v2, /device:TPU:0, one launch (start us, length us, event | category | flops | bytes accessed | tf_op | source)
XLA Modules:
  0.0 179.0 jit_solution(10999279289571162823)
XLA Ops:
  0.6 89.8 %front.1 = (f32[1,128]{1,0:T(1,128)}, bf16[32,192,128]{2,1,0:T(8,128)(2,1)}, bf16[32,64,128]{2,1,0:T(8,128)(2,1)}) custom-call(bf16[128,2432]{1,0:T(8,128)(2,1)} %bitcast.12, bf16[128,2432]{1,0:T(8,128)(2,1)} %bitcast.13, bf16[128,2048]{1,0:T(8,128)(2,1)} %bitcast.14, bf16[128,2048]{1,0:T(8,128)(2,1)} %bitcast.15, bf16[128,2048]{1,0:T(8,128)(2,1)} %bitcast.16, ...), custom_call_target="tpu_custom_call" | custom-call | tf_op jit(solution)/shard_map/front/pallas_call | solution.py:275
  90.4 0.0 copy-start.1
  90.4 58.4 %attention.1.o_ref = bf16[32,192,128]{2,1,0:T(8,128)(2,1)} custom-call(bf16[32,192,128]{2,1,0:T(8,128)(2,1)} %get-tuple-element.11.x_ref, bf16[32,64,128]{2,1,0:T(8,128)(2,1)} %get-tuple-element.12.g_ref), custom_call_target="tpu_custom_call" | custom-call | tf_op jit(solution)/shard_map/attention/pallas_call | solution.py:85
  148.8 0.0 copy-start
  148.9 1.4 copy-done
  150.3 25.8 %back.1 = (bf16[128,2048]{1,0:T(8,128)(2,1)S(1)}, bf16[128,2048]{1,0:T(8,128)(2,1)S(1)}, bf16[128,2048]{1,0:T(8,128)(2,1)S(1)}) custom-call(bf16[32,192,128]{2,1,0:T(8,128)(2,1)S(1)} %copy-done), custom_call_target="tpu_custom_call" | custom-call | tf_op jit(solution)/shard_map/back/pallas_call | solution.py:305
  176.1 0.0 copy-done.1
  176.1 0.5 copy.17
  176.6 0.8 copy.18
  177.4 0.8 copy.19
  178.2 0.8 copy.20
Async XLA Ops:
  90.4 85.7 %copy-start.1 = (f32[1,128]{1,0:T(1,128)S(1)}, f32[1,128]{1,0:T(1,128)}, u32[]{:S(2)}) copy-start(f32[1,128]{1,0:T(1,128)} %get-tuple-element.20) | copy-start | bytes 1540
  148.8 1.4 copy-start

commit v3 on v2

v3 whole, which is shorter than its diff:
```python
import jax
import jax.numpy as jnp
from jax import lax
from jax.experimental import pallas as pl
from jax.experimental.pallas import tpu as pltpu
from jax.sharding import PartitionSpec as P

LOG2E = 1.4426950408889634
F32=jnp.float32; BF=jnp.bfloat16
QB=256; KC=256; QP=512; KB=512; L=4096; NB=32; HD=64
T=128; D=2432; HID=1024; C=1536
NQ=L//QB
MESH=pl.DeviceIdType.MESH
LOSS_WEIGHT=1000.0

def dot(a,b): return jnp.dot(a,b,preferred_element_type=F32)
def dot_nt(a,b): return lax.dot_general(a,b,(((1,),(1,)),((),())),preferred_element_type=F32)

def scores_prep(x,kk,vt):
    for j in range(NB):
        rows=pl.ds(j*T,T)
        kn=x[j,HD:2*HD].T
        kk[rows,:]=jnp.concatenate([kn,kn],axis=1)
        vt[pl.ds(0,HD),rows]=x[j,2*HD:]
    vt[pl.ds(HD,16),:]=jnp.ones((16,L),BF)


def stage(i,x,kk,vt,sn,so,m,u_ref,a_ref,first=False,last=False):
    per=QB//T
    if not last:
        qt=jnp.concatenate([x[i*per+j,:HD] for j in range(per)],axis=1)
        qf=qt.astype(F32)*(0.125*LOG2E)
        qhi=qf.astype(BF); qlo=(qf-qhi.astype(F32)).astype(BF)
        qa=jnp.concatenate([qhi,qlo],axis=0)
    mn=jnp.full((8,QB),-jnp.inf,F32)
    acc=jnp.zeros((HD+16,QB),F32)
    for c in range(L//KC):
        rows=pl.ds(c*KC,KC)
        if not last:
            y=dot(kk[rows,:],qa)
            sn[rows,:]=y
            mn=jnp.maximum(mn,jnp.max(y.reshape(KC//8,8,QB),axis=0))
        if not first:
            u=jnp.exp2(so[rows,:]-m).astype(BF)
            u_ref[rows,:]=u
            acc=acc+dot(vt[:,rows],u)
    if not first:
        j=i-1
        a_ref[:,pl.ds(j*QB if isinstance(j,int) else pl.multiple_of(j*QB,QB),QB)]=acc
    return jnp.max(mn,axis=0,keepdims=True)


def grads_prep(x,g_ref,a_ref,vv,kt,ga,qn,gn,rlr):
    lane=lax.broadcasted_iota(jnp.int32,(T,HD),1)
    ones=jnp.where(lane<2,1.0,0.0).astype(BF)
    row=lax.broadcasted_iota(jnp.int32,(HD,T),0)
    for j in range(NB):
        rows=pl.ds(j*T,T)
        vv[rows,:]=jnp.concatenate([x[j,2*HD:].T,ones],axis=1)
        kt[:,rows]=x[j,HD:2*HD]*BF(0.125)
        a=a_ref[:,rows]
        rl=1.0/a[HD:HD+1]
        rlr[0:1,rows]=rl
        gt=g_ref[j]; gf=gt.astype(F32)
        d=-jnp.sum(gf*a[:HD],axis=0,keepdims=True)*rl
        dhi=d.astype(BF); dlo=d-dhi.astype(F32)
        ga[pl.ds(0,HD),rows]=gt
        ga[pl.ds(HD,HD),rows]=jnp.where(row==0,dhi.astype(F32),jnp.where(row==1,dlo,0.0)).astype(BF)
        qn[rows,:]=(x[j,:HD].astype(F32)*(rl*0.125)).T.astype(BF)
        gn[rows,:]=(gf*rl).T.astype(BF)


def remote(src,dst,send,recv,dev):
    return pltpu.make_async_remote_copy(src_ref=src,dst_ref=dst,send_sem=send,recv_sem=recv,device_id=dev,device_id_type=MESH)


def wait_bytes(ref,sem):
    pltpu.make_async_copy(ref,ref,sem).wait()


def greet(dp,seq,extra):
    barrier=pltpu.get_barrier_semaphore()
    def hello(r,c):
        pl.semaphore_signal(barrier,inc=1,device_id=(dp,lax.rem(seq+r,NB)),device_id_type=MESH)
        return c
    lax.fori_loop(1,NB,hello,0)
    for dev in extra:
        pl.semaphore_signal(barrier,inc=1,device_id=dev,device_id_type=MESH)


def meet(extra):
    pl.semaphore_wait(pltpu.get_barrier_semaphore(),NB-1+extra)


def front_kernel(hid,cot,q,k,v,wi_h,wo_h,wa_h,dino, cos_o,x_o,g_o,u_o,a_o,
        wi,wo,wa,xt,gt,feat,X,Z,pre,sil,p1s,p1c,p1p,p1r,p1q,p2s,p2c,p2p,p2r,p2q,
        xh,kk,vt,sa,sb,ua,ub,wsem,xsem,fsem,gsem,hs,hr,zs,zr,s1,r1,s2,r2,usem,osem):
    dp=lax.axis_index("dp"); seq=lax.axis_index("seq")
    core=lax.rem(dp,2); hi=dp//2
    partner=(hi*2+(1-core),seq)
    cross_seq=lax.rem(seq+NB//2,NB)
    cross=((1-hi)*2+core,cross_seq)
    diag=((1-hi)*2+(1-core),cross_seq)
    loads=[pltpu.make_async_copy(a,b,wsem.at[n]) for n,(a,b) in enumerate(((wi_h,wi),(wo_h,wo),(wa_h,wa)))]
    for ld in loads: ld.start()
    greet(dp,seq,(partner,cross))
    meet(2)
    H=T//2
    def half(ref,h): return ref.at[pl.ds(h*H,H)]
    def ucopy(i,n): return pltpu.make_async_copy((ua,ub)[n],u_o.at[i],usem.at[n])
    def pairs(lo,hi_,m):
        def body(p,m):
            i=2*p+1
            @pl.when(p>0)
            def _(): ucopy(0,0).wait()
            m=stage(i,xh,kk,vt,sb,sa,m,ua,a_o)
            ucopy(i-1,0).start()
            @pl.when(p>0)
            def _(): ucopy(0,1).wait()
            m=stage(i+1,xh,kk,vt,sa,sb,m,ub,a_o)
            ucopy(i,1).start()
            return m
        return lax.fori_loop(lo,hi_,body,m)
    hc=[remote(half(hid,h),X.at[2,pl.ds(h*H,H)],hs.at[h],hr.at[h],cross) for h in range(2)]
    hp=remote(hid,X.at[1],hs.at[2],hr.at[2],partner)
    hf=[remote(X.at[2,pl.ds(h*H,H)],X.at[3,pl.ds(h*H,H)],hs.at[3+h],hr.at[3+h],partner) for h in range(2)]
    for c in hc: c.start()
    hp.start()
    def send_feat(r,c):
        peer=lax.rem(seq+r,NB)
        remote(dino.at[:,pl.ds(pl.multiple_of(peer*T,T),T)],feat.at[seq],fsem.at[0],fsem.at[1],(dp,peer)).start()
        return c
    pltpu.make_async_copy(dino.at[:,pl.ds(pl.multiple_of(seq*T,T),T)],feat.at[seq],fsem.at[1]).start()
    def turn(p):
        cols=pl.ds(pl.multiple_of(p*T,T),T)
        for n,ref in enumerate((q,k,v)):
            t=ref[:,cols].T
            xt[2*p,pl.ds(n*HD,HD)]=t[:HD]
            xt[2*p+1,pl.ds(n*HD,HD)]=t[HD:]
    base=seq//2
    turn(base)
    pltpu.make_async_copy(xt.at[seq],xh.at[seq],xsem.at[1]).start()
    mate=base*2+(1-lax.rem(seq,2))
    remote(xt.at[mate],xh.at[seq],xsem.at[0],xsem.at[1],(dp,mate)).start()
    def turn_send(i,c):
        p=lax.rem(base+i,NB//2)
        turn(p)
        for e in range(2):
            remote(xt.at[2*p+e],xh.at[seq],xsem.at[0],xsem.at[1],(dp,2*p+e)).start()
        return c
    lax.fori_loop(1,NB//2,turn_send,0)
    lax.fori_loop(1,NB,send_feat,0)
    X[0]=hid[...]
    loads[0].wait()
    hp.wait_recv()
    def first(at,rows):
        def body(n,c):
            cols=pl.ds(pl.multiple_of(n*256,256),256)
            y=dot(X[at:at+2].reshape(2*T,D),wi[:,cols])
            pre[pl.ds(rows,2*T),cols]=y
            sil[pl.ds(rows,2*T),cols]=(y/(1.0+jnp.exp(-y))).astype(BF)
            return c
        lax.fori_loop(0,HID//256,body,0)
    first(0,0)
    for h in range(2):
        hc[h].wait_recv(); hf[h].start()
    for h in range(2): hf[h].wait_recv()
    first(2,2*T)
    loads[1].wait()
    def second(n,c):
        cols=pl.ds(pl.multiple_of(n*256,256),256)
        y=dot(sil[2*T:],wo[:,cols])
        p1c[:,cols]=y[:T]
        p1s[0,:,cols]=y[T:].astype(BF)
        return c
    lax.fori_loop(0,C//256,second,0)
    c1=remote(p1s.at[0],p1r.at[0],s1.at[0],r1.at[0],partner); c1.start()
    def second_own(n,c):
        cols=pl.ds(pl.multiple_of(n*256,256),256)
        y=dot(sil[:2*T],wo[:,cols])
        p1q[:,cols]=y[:T]
        p1s[1,:,cols]=y[T:].astype(BF)
        return c
    lax.fori_loop(0,C//256,second_own,0)
    c2=remote(p1s.at[1],p1r.at[1],s1.at[1],r1.at[1],partner); c2.start()
    c1.wait_recv()
    p1p[...]=(p1c[...]+p1r[0].astype(F32)).astype(BF)
    c3=remote(p1p,p1r.at[2],s1.at[2],r1.at[2],cross); c3.start()
    wait_bytes(feat,fsem.at[1])
    f=feat[...].astype(F32)
    mean=jnp.sum(jnp.sum(f,axis=0),axis=0,keepdims=True)*(1.0/C)
    sh=f-mean[None]
    var=jnp.sum(jnp.sum(sh*sh,axis=0),axis=0,keepdims=True)*(1.0/C)
    sh=sh*lax.rsqrt(var+1e-6)[None]
    nn=jnp.sum(jnp.sum(sh*sh,axis=0),axis=0,keepdims=True)
    sh=sh*lax.rsqrt(nn+1e-6)[None]
    target=sh.reshape(C,T).T
    wait_bytes(xh,xsem.at[1])
    xcopy=pltpu.make_async_copy(xh,x_o,osem); xcopy.start()
    scores_prep(xh,kk,vt)
    m=stage(0,xh,kk,vt,sa,None,None,None,None,first=True)
    m=pairs(0,2,m)
    c2.wait_recv(); c3.wait_recv()
    pr=p1q[...]+p1r[1].astype(F32)+p1r[2].astype(F32)
    rinv=lax.rsqrt(jnp.sum(pr*pr,axis=1,keepdims=True)+1e-6)
    direction=pr*rinv
    cosine=jnp.sum(direction*target,axis=1,keepdims=True)
    ii=lax.broadcasted_iota(jnp.int32,(T,T),0); jj=lax.broadcasted_iota(jnp.int32,(T,T),1)
    cos_o[...]=jnp.sum(jnp.where(ii==jj,cosine,0.0),axis=0,keepdims=True)
    Z[0]=(-LOSS_WEIGHT*rinv*(target-cosine*direction)).astype(BF)
    zc=[remote(Z.at[0,pl.ds(h*H,H)],Z.at[2,pl.ds(h*H,H)],zs.at[h],zr.at[h],cross) for h in range(2)]
    zp=remote(Z.at[0],Z.at[1],zs.at[2],zr.at[2],partner)
    zf=[remote(Z.at[2,pl.ds(h*H,H)],Z.at[3,pl.ds(h*H,H)],zs.at[3+h],zr.at[3+h],partner) for h in range(2)]
    for c in zc: c.start()
    zp.start()
    zp.wait_recv()
    def back(at,rows):
        def body(n,c):
            cols=pl.ds(pl.multiple_of(n*256,256),256)
            gs=dot_nt(Z[at:at+2].reshape(2*T,C),wo[cols,:])
            y=pre[pl.ds(rows,2*T),cols]
            s=1.0/(1.0+jnp.exp(-y))
            sil[pl.ds(rows,2*T),cols]=(gs*(s*(1.0+y*(1.0-s)))).astype(BF)
            return c
        lax.fori_loop(0,HID//256,body,0)
    back(0,0)
    m=pairs(2,3,m)
    for h in range(2):
        zc[h].wait_recv(); zf[h].start()
        m=pairs(3+h,4+h,m)
    for h in range(2): zf[h].wait_recv()
    back(2,2*T)
    def third(n,c):
        cols=pl.ds(pl.multiple_of(n*128,128),128)
        y=dot_nt(sil[2*T:],wi[cols,:])
        p2c[:,cols]=y[:T]
        p2s[0,:,cols]=y[T:].astype(BF)
        return c
    lax.fori_loop(0,D//128,third,0)
    d1=remote(p2s.at[0],p2r.at[0],s2.at[0],r2.at[0],partner); d1.start()
    def third_own(n,c):
        cols=pl.ds(pl.multiple_of(n*128,128),128)
        y=dot_nt(sil[:2*T],wi[cols,:])
        p2q[:,cols]=y[:T]
        p2s[1,:,cols]=y[T:].astype(BF)
        return c
    d1.wait_recv()
    p2p[...]=(p2c[...]+p2r[0].astype(F32)).astype(BF)
    d3=remote(p2p,p2r.at[2],s2.at[2],r2.at[2],cross); d3.start()
    lax.fori_loop(0,D//128,third_own,0)
    d2=remote(p2s.at[1],p2r.at[1],s2.at[1],r2.at[1],partner); d2.start()
    m=pairs(5,7,m)
    ucopy(0,0).wait()
    m=stage(NQ-1,xh,kk,vt,sb,sa,m,ua,a_o)
    ucopy(NQ-2,0).start()
    ucopy(0,1).wait()
    stage(NQ,xh,kk,vt,None,sb,m,ub,a_o,last=True)
    ucopy(NQ-1,1).start()
    loads[2].wait()
    d2.wait_recv(); d3.wait_recv()
    gh=(cot[...].astype(F32)+(p2q[...]+p2r[1].astype(F32)+p2r[2].astype(F32))).astype(BF)
    R=512
    def heads(i,c):
        at=lax.rem(seq//8+i,L//2//R)
        y=dot_nt(wa[pl.ds(pl.multiple_of(at*R,R),R)],Z2[...]).astype(BF)
        gt[pl.ds(at*8,8)]=y.reshape(8,HD,T)
        for e in range(8):
            h=at*8+lax.rem(seq+e,8)
            @pl.when(h!=seq)
            def _():
                remote(gt.at[h],g_o.at[seq],gsem.at[0],gsem.at[1],(dp,h)).start()
            @pl.when(h==seq)
            def _():
                pltpu.make_async_copy(gt.at[h],g_o.at[seq],gsem.at[1]).start()
        return c
    Z2=X.at[0]
    X[0]=gh
    lax.fori_loop(0,4,heads,0)
    xcopy.wait()
    for n in range(2): ucopy(n,n).wait()
    for c in hc+[hp]+hf+zc+[zp]+zf+[c1,c2,c3,d1,d2,d3]: c.wait_send()
    wait_bytes(xt.at[pl.ds(0,NB-1)],xsem.at[0])
    wait_bytes(feat.at[pl.ds(0,NB-1)],fsem.at[0])
    wait_bytes(g_o,gsem.at[1]); wait_bytes(gt.at[pl.ds(0,NB-1)],gsem.at[0])


def front(hid,cot,q,k,v,wi,wo,wa,dino):
    vm=pl.BlockSpec(memory_space=pltpu.VMEM); hb=pl.BlockSpec(memory_space=pl.ANY)
    V=pltpu.VMEM; S=pltpu.SemaphoreType.DMA
    return pl.pallas_call(front_kernel,
        in_specs=[vm]*5+[hb]*3+[vm],out_specs=[vm,hb,hb,hb,vm],
        out_shape=[jax.ShapeDtypeStruct((1,T),F32),jax.ShapeDtypeStruct((NB,3*HD,T),BF),jax.ShapeDtypeStruct((NB,HD,T),BF),
            jax.ShapeDtypeStruct((NQ,L,QB),BF),jax.ShapeDtypeStruct((HD+16,L),F32)],
        scratch_shapes=[V((D,HID),BF),V((HID,C),BF),V((2048,D),BF),V((NB,3*HD,T),BF),V((NB,HD,T),BF),V((NB,48,T),BF),
            V((4,T,D),BF),V((4,T,C),BF),V((4*T,HID),F32),V((4*T,HID),BF),
            V((2,T,C),BF),V((T,C),F32),V((T,C),BF),V((3,T,C),BF),V((T,C),F32),
            V((2,T,D),BF),V((T,D),F32),V((T,D),BF),V((3,T,D),BF),V((T,D),F32),
            V((NB,3*HD,T),BF),V((L,T),BF),V((HD+16,L),BF),V((L,QB),F32),V((L,QB),F32),V((L,QB),BF),V((L,QB),BF),
            S((3,)),S((2,)),S((2,)),S((2,)),S((5,)),S((5,)),S((5,)),S((5,)),S((3,)),S((3,)),S((3,)),S((3,)),S((2,)),S],
        compiler_params=pltpu.CompilerParams(collective_id=0,has_side_effects=True,vmem_limit_bytes=62*2**20),
        name="front")(hid,cot,q,k,v,wi,wo,wa,dino)


def finish_kernel(x_ref,g_ref,a_ref,u_h,q_o,k_o,v_o,vv,kt,ga,qn,gn,rlr,dq,u_ref,o_ref,buf,usem,ksem,qsem):
    dp=lax.axis_index("dp"); seq=lax.axis_index("seq")
    NK=L//KB; per=KB//T
    first=seq//per
    def place(b): return lax.rem(b+first,NK)
    def fetch(b):
        slot=lax.rem(b,2)
        return pltpu.make_async_copy(u_h.at[:,pl.ds(pl.multiple_of(place(b)*KB,KB),KB)],u_ref.at[slot],usem.at[slot])
    fetch(0).start()
    greet(dp,seq,())
    grads_prep(x_ref,g_ref,a_ref,vv,kt,ga,qn,gn,rlr)
    dq[...]=jnp.zeros_like(dq)
    meet(0)
    def give(h,part,sem):
        @pl.when(h!=seq)
        def _():
            remote(o_ref.at[h,part],buf.at[seq,part],sem.at[0],sem.at[1],(dp,h)).start()
        @pl.when(h==seq)
        def _():
            pltpu.make_async_copy(o_ref.at[h,part],buf.at[seq,part],sem.at[1]).start()
    def body(b,c):
        slot=lax.rem(b,2)
        @pl.when(b<NK-1)
        def _(): fetch(b+1).start()
        fetch(b).wait()
        at=place(b)
        kr=pl.ds(pl.multiple_of(at*KB,KB),KB)
        v=vv[kr,:]; k=kt[:,kr]
        dk=jnp.zeros((KB,HD),F32); dv=jnp.zeros((KB,HD),F32)
        for i in range(L//QP):
            qr=pl.ds(i*QP,QP)
            n=QP//QB
            u=jnp.concatenate([u_ref[slot,i*n+e] for e in range(n)],axis=1)
            ds=(u.astype(F32)*dot(v,ga[:,qr])).astype(BF)
            dk=dk+dot(ds,qn[qr,:]); dv=dv+dot(u,gn[qr,:])
            dq[:,qr]+=dot(k,ds)
        for j in range(per):
            o_ref[at*per+j,HD:2*HD]=dk[j*T:(j+1)*T].T.astype(BF)
            o_ref[at*per+j,2*HD:]=dv[j*T:(j+1)*T].T.astype(BF)
        for j in range(per):
            give(at*per+lax.rem(seq+j,per),pl.ds(HD,2*HD),ksem)
        return c
    lax.fori_loop(0,NK,body,0)
    for j in range(NB):
        o_ref[j,:HD]=(dq[:,j*T:(j+1)*T]*rlr[0:1,j*T:(j+1)*T]).astype(BF)
    def send(r,c):
        give(lax.rem(seq+r,NB),pl.ds(0,HD),qsem)
        return c
    lax.fori_loop(0,NB,send,0)
    kpart=buf.at[:,pl.ds(HD,2*HD)]
    wait_bytes(kpart,ksem.at[1])
    def out(ref,n):
        for p in range(NB//2):
            ref[:,p*T:(p+1)*T]=buf[2*p:2*p+2,n*HD:(n+1)*HD].reshape(T,T).T
    out(k_o,1); out(v_o,2)
    qpart=buf.at[:,pl.ds(0,HD)]
    wait_bytes(qpart,qsem.at[1])
    out(q_o,0)
    wait_bytes(buf.at[pl.ds(0,NB-1),pl.ds(HD,2*HD)],ksem.at[0])
    wait_bytes(buf.at[pl.ds(0,NB-1),pl.ds(0,HD)],qsem.at[0])


def finish(x,g,u,a):
    V=pltpu.VMEM; S=pltpu.SemaphoreType.DMA
    vm=pl.BlockSpec(memory_space=V); hb=pl.BlockSpec(memory_space=pl.ANY)
    return pl.pallas_call(finish_kernel,in_specs=[vm]*3+[hb],out_specs=[vm]*3,
        out_shape=[jax.ShapeDtypeStruct((T,NB*HD),BF)]*3,
        scratch_shapes=[V((L,T),BF),V((HD,L),BF),V((T,L),BF),V((L,HD),BF),V((L,HD),BF),V((8,L),F32),V((HD,L),F32),
            V((2,NQ,KB,QB),BF),V((NB,3*HD,T),BF),V((NB,3*HD,T),BF),S((2,)),S((2,)),S((2,))],
        compiler_params=pltpu.CompilerParams(collective_id=1,has_side_effects=True,vmem_limit_bytes=56*2**20),
        name="finish")(x,g,a,u)


def on_device(hidden,out_cot,proj_in,proj_out,attn_out_w,queries,keys,values,dino):
    cosine,x,g,u,a=front(hidden[0],out_cot[0],queries[0],keys[0],values[0],proj_in,proj_out,attn_out_w,dino[0])
    gq,gk,gv=finish(x,g,u,a)
    return cosine,gq[None],gk[None],gv[None]


def solution(mesh):
    in_specs = (
        P("dp", "seq", None),
        P("dp", "seq", None),
        P(None, "dp"),
        P("dp", None),
        P(),
        P("dp", "seq", None),
        P("dp", "seq", None),
        P("dp", "seq", None),
        P("dp", "seq", None),
    )
    out_specs = (P("dp", "seq"), P("dp", "seq", None), P("dp", "seq", None), P("dp", "seq", None))
    return jax.shard_map(
        on_device, mesh=mesh, in_specs=in_specs, out_specs=out_specs, check_vma=False
    )
```

time: 179 us -> 154 us (0.86)
  Pallas kernels: 174 us -> 147 us
  local copies, waits for them, and re-layouts: 4.3 us -> 6.16 us
    pallas_call x2 -> x1, Pallas kernels: 84.2 us -> 51.1 us  [finish(): pl.pallas_call(finish_kernel, in_specs=[vm] * 3 + [hb], out_specs=[vm] *...]
    pallas_call x1, Pallas kernels: 89.8 us -> 95.5 us  [front(): pl.pallas_call(front_kernel, in_specs=[vm] * 5 + [hb] * 3 + [vm], out_spe...]
    unnamed x8 -> x6, local copies, waits for them, and re-layouts: 4.3 us -> 6.16 us
where the time goes in v3:
time: 154 us; the launch traced here: 153 us
  Pallas kernels  147 us (95%)
  local copies, waits for them, and re-layouts  6.16 us (4%)
    pallas_call x1, Pallas kernels, front(): pl.pallas_call(front_kernel, in_specs=[vm] * 5 + [hb] * 3 + [vm], out_spe...  95.5 us
    pallas_call x1, Pallas kernels, finish(): pl.pallas_call(finish_kernel, in_specs=[vm] * 3 + [hb], out_specs=[vm] *...  51.1 us
    unnamed x6, local copies, waits for them, and re-layouts  6.16 us

profile of v3, /device:TPU:0, one launch (start us, length us, event | category | flops | bytes accessed | tf_op | source)
XLA Modules:
  0.0 153.5 jit_solution(7181670159079993040)
XLA Ops:
  0.6 95.5 %front.1 = (f32[1,128]{1,0:T(1,128)}, bf16[32,192,128]{2,1,0:T(8,128)(2,1)}, bf16[32,64,128]{2,1,0:T(8,128)(2,1)}, bf16[16,4096,256]{2,1,0:T(8,128)(2,1)}, f32[80,4096]{1,0:T(8,128)}) custom-call(bf16[128,2432]{1,0:T(8,128)(2,1)} %bitcast.9, bf16[128,2432]{1,0:T(8,128)(2,1)} %bitcast.10, bf16[128,2048]{1,0:T(8,128)(2,1)} %bitcast.14, ...), custom_call_target="tpu_custom_call" | custom-call | tf_op jit(solution)/shard_map/front/pallas_call | solution.py:290
  96.1 0.0 copy-start
  96.1 51.1 %finish.1 = (bf16[128,2048]{1,0:T(8,128)(2,1)}, bf16[128,2048]{1,0:T(8,128)(2,1)}, bf16[128,2048]{1,0:T(8,128)(2,1)}) custom-call(bf16[32,192,128]{2,1,0:T(8,128)(2,1)} %get-tuple-element.13.x_ref, bf16[32,64,128]{2,1,0:T(8,128)(2,1)} %get-tuple-element.14.g_ref, f32[80,4096]{1,0:T(8,128)} %get-tuple-element.15.a_ref, ...), custom_call_target="tpu_custom_call" | custom-call | tf_op jit(solution)/shard_map/finish/pallas_call | solution.py:369
  147.3 0.0 copy-done
  147.3 0.5 copy.17
  147.8 1.9 %copy.18 = bf16[1,128,2048]{2,1,0:T(8,128)(2,1)} copy(bf16[1,128,2048]{2,1,0:T(8,128)(2,1)} %bitcast.13) | data formatting | bytes 1048576
  149.7 1.9 %copy.19 = bf16[1,128,2048]{2,1,0:T(8,128)(2,1)} copy(bf16[1,128,2048]{2,1,0:T(8,128)(2,1)} %bitcast.12) | data formatting | bytes 1048576
  151.6 1.9 %copy.20 = bf16[1,128,2048]{2,1,0:T(8,128)(2,1)} copy(bf16[1,128,2048]{2,1,0:T(8,128)(2,1)} %bitcast.11) | data formatting | bytes 1048576
Async XLA Ops:
  96.1 51.2 %copy-start = (f32[1,128]{1,0:T(1,128)S(1)}, f32[1,128]{1,0:T(1,128)}, u32[]{:S(2)}) copy-start(f32[1,128]{1,0:T(1,128)} %get-tuple-element.24) | copy-start | bytes 1540

commit v4 on v3

--- a/solution.py
+++ b/solution.py
@@ -93,7 +93,7 @@
 
 
 def front_kernel(hid,cot,q,k,v,wi_h,wo_h,wa_h,dino, cos_o,x_o,g_o,u_o,a_o,
-        wi,wo,wa,xt,gt,feat,X,Z,pre,sil,p1s,p1c,p1p,p1r,p1q,p2s,p2c,p2p,p2r,p2q,
+        wi,wo,wa,xt,gt,feat,X,Z,pre,sil,p1s,p1c,p1p,p1r,p1q,p2s,p2c,p2p,p2r,p2q,target,gh,
         xh,kk,vt,sa,sb,ua,ub,wsem,xsem,fsem,gsem,hs,hr,zs,zr,s1,r1,s2,r2,usem,osem):
     dp=lax.axis_index("dp"); seq=lax.axis_index("seq")
     core=lax.rem(dp,2); hi=dp//2
@@ -106,7 +106,6 @@
     greet(dp,seq,(partner,cross))
     meet(2)
     H=T//2
-    def half(ref,h): return ref.at[pl.ds(h*H,H)]
     def ucopy(i,n): return pltpu.make_async_copy((ua,ub)[n],u_o.at[i],usem.at[n])
     def pairs(lo,hi_,m):
         def body(p,m):
@@ -121,16 +120,16 @@
             ucopy(i,1).start()
             return m
         return lax.fori_loop(lo,hi_,body,m)
-    hc=[remote(half(hid,h),X.at[2,pl.ds(h*H,H)],hs.at[h],hr.at[h],cross) for h in range(2)]
-    hp=remote(hid,X.at[1],hs.at[2],hr.at[2],partner)
-    hf=[remote(X.at[2,pl.ds(h*H,H)],X.at[3,pl.ds(h*H,H)],hs.at[3+h],hr.at[3+h],partner) for h in range(2)]
-    for c in hc: c.start()
-    hp.start()
+    hc=[remote(hid.at[pl.ds(h*H,H)],X.at[h,2],hs.at[h],hr.at[h],cross) for h in range(2)]
+    hp=[remote(hid.at[pl.ds(h*H,H)],X.at[h,1],hs.at[2+h],hr.at[2+h],partner) for h in range(2)]
+    hf=[remote(X.at[h,2],X.at[h,3],hs.at[4+h],hr.at[4+h],partner) for h in range(2)]
+    hc[0].start(); hp[0].start(); hc[1].start(); hp[1].start()
     def send_feat(r,c):
         peer=lax.rem(seq+r,NB)
         remote(dino.at[:,pl.ds(pl.multiple_of(peer*T,T),T)],feat.at[seq],fsem.at[0],fsem.at[1],(dp,peer)).start()
         return c
     pltpu.make_async_copy(dino.at[:,pl.ds(pl.multiple_of(seq*T,T),T)],feat.at[seq],fsem.at[1]).start()
+    lax.fori_loop(1,NB,send_feat,0)
     def turn(p):
         cols=pl.ds(pl.multiple_of(p*T,T),T)
         for n,ref in enumerate((q,k,v)):
@@ -149,43 +148,48 @@
             remote(xt.at[2*p+e],xh.at[seq],xsem.at[0],xsem.at[1],(dp,2*p+e)).start()
         return c
     lax.fori_loop(1,NB//2,turn_send,0)
-    lax.fori_loop(1,NB,send_feat,0)
-    X[0]=hid[...]
-    loads[0].wait()
-    hp.wait_recv()
-    def first(at,rows):
+    def first(h):
         def body(n,c):
             cols=pl.ds(pl.multiple_of(n*256,256),256)
-            y=dot(X[at:at+2].reshape(2*T,D),wi[:,cols])
-            pre[pl.ds(rows,2*T),cols]=y
-            sil[pl.ds(rows,2*T),cols]=(y/(1.0+jnp.exp(-y))).astype(BF)
+            y=dot(X[h].reshape(4*H,D),wi[:,cols])
+            pre[h,:,cols]=y
+            sil[h,:,cols]=(y/(1.0+jnp.exp(-y))).astype(BF)
             return c
         lax.fori_loop(0,HID//256,body,0)
-    first(0,0)
-    for h in range(2):
-        hc[h].wait_recv(); hf[h].start()
-    for h in range(2): hf[h].wait_recv()
-    first(2,2*T)
+    def second(h):
+        def body(n,c):
+            cols=pl.ds(pl.multiple_of(n*256,256),256)
+            y=dot(sil[h],wo[:,cols])
+            p1q[h,:,cols]=y[:H]
+            p1s[h,1,:,cols]=y[H:2*H].astype(BF)
+            p1c[h,:,cols]=y[2*H:3*H]
+            p1s[h,0,:,cols]=y[3*H:].astype(BF)
+            return c
+        lax.fori_loop(0,C//256,body,0)
+    def trio(sent,summed,recv,ss,rs):
+        return [[remote(sent.at[h,0],recv.at[h,0],ss.at[h,0],rs.at[h,0],partner),
+            remote(sent.at[h,1],recv.at[h,1],ss.at[h,1],rs.at[h,1],partner),
+            remote(summed.at[h],recv.at[h,2],ss.at[h,2],rs.at[h,2],cross)] for h in range(2)]
+    cs=trio(p1s,p1p,p1r,s1,r1)
+    ds=trio(p2s,p2p,p2r,s2,r2)
+    def pass_on(h,tr,own,recv,summed):
+        tr[h][0].wait_recv()
+        summed[h]=(own[h]+recv[h,0].astype(F32)).astype(BF)
+        tr[h][2].start()
+    for h in range(2): X[h,0]=hid[h*H:(h+1)*H]
+    hc[0].wait_recv(); hf[0].start()
+    loads[0].wait()
+    hp[0].wait_recv(); hf[0].wait_recv()
+    first(0)
+    hc[1].wait_recv(); hf[1].start()
     loads[1].wait()
-    def second(n,c):
-        cols=pl.ds(pl.multiple_of(n*256,256),256)
-        y=dot(sil[2*T:],wo[:,cols])
-        p1c[:,cols]=y[:T]
-        p1s[0,:,cols]=y[T:].astype(BF)
-        return c
-    lax.fori_loop(0,C//256,second,0)
-    c1=remote(p1s.at[0],p1r.at[0],s1.at[0],r1.at[0],partner); c1.start()
-    def second_own(n,c):
-        cols=pl.ds(pl.multiple_of(n*256,256),256)
-        y=dot(sil[:2*T],wo[:,cols])
-        p1q[:,cols]=y[:T]
-        p1s[1,:,cols]=y[T:].astype(BF)
-        return c
-    lax.fori_loop(0,C//256,second_own,0)
-    c2=remote(p1s.at[1],p1r.at[1],s1.at[1],r1.at[1],partner); c2.start()
-    c1.wait_recv()
-    p1p[...]=(p1c[...]+p1r[0].astype(F32)).astype(BF)
-    c3=remote(p1p,p1r.at[2],s1.at[2],r1.at[2],cross); c3.start()
+    second(0)
+    cs[0][0].start(); cs[0][1].start()
+    hp[1].wait_recv(); hf[1].wait_recv()
+    first(1)
+    pass_on(0,cs,p1c,p1r,p1p)
+    second(1)
+    cs[1][0].start(); cs[1][1].start()
     wait_bytes(feat,fsem.at[1])
     f=feat[...].astype(F32)
     mean=jnp.sum(jnp.sum(f,axis=0),axis=0,keepdims=True)*(1.0/C)
@@ -194,75 +198,74 @@
     sh=sh*lax.rsqrt(var+1e-6)[None]
     nn=jnp.sum(jnp.sum(sh*sh,axis=0),axis=0,keepdims=True)
     sh=sh*lax.rsqrt(nn+1e-6)[None]
-    target=sh.reshape(C,T).T
+    target[...]=sh.reshape(C,T).T
+    pass_on(1,cs,p1c,p1r,p1p)
+    zc=[remote(Z.at[h,0],Z.at[h,2],zs.at[h],zr.at[h],cross) for h in range(2)]
+    zp=[remote(Z.at[h,0],Z.at[h,1],zs.at[2+h],zr.at[2+h],partner) for h in range(2)]
+    zf=[remote(Z.at[h,2],Z.at[h,3],zs.at[4+h],zr.at[4+h],partner) for h in range(2)]
+    ii=lax.broadcasted_iota(jnp.int32,(H,T),0); jj=lax.broadcasted_iota(jnp.int32,(H,T),1)
+    rows_of=[]
+    def loss(h):
+        cs[h][1].wait_recv(); cs[h][2].wait_recv()
+        tg=target[h*H:(h+1)*H]
+        pr=p1q[h]+p1r[h,1].astype(F32)+p1r[h,2].astype(F32)
+        rinv=lax.rsqrt(jnp.sum(pr*pr,axis=1,keepdims=True)+1e-6)
+        direction=pr*rinv
+        cosine=jnp.sum(direction*tg,axis=1,keepdims=True)
+        rows_of.append(jnp.sum(jnp.where(ii+h*H==jj,cosine,0.0),axis=0,keepdims=True))
+        Z[h,0]=(-LOSS_WEIGHT*rinv*(tg-cosine*direction)).astype(BF)
+        zc[h].start(); zp[h].start()
+    loss(0)
+    loss(1)
+    cos_o[...]=rows_of[0]+rows_of[1]
+    def slope(h):
+        zp[h].wait_recv(); zf[h].wait_recv()
+        def body(n,c):
+            cols=pl.ds(pl.multiple_of(n*256,256),256)
+            gs=dot_nt(Z[h].reshape(4*H,C),wo[cols,:])
+            y=pre[h,:,cols]
+            s=1.0/(1.0+jnp.exp(-y))
+            sil[h,:,cols]=(gs*(s*(1.0+y*(1.0-s)))).astype(BF)
+            return c
+        lax.fori_loop(0,HID//256,body,0)
+    def third(h):
+        def part(cols):
+            y=dot_nt(sil[h],wi[cols,:])
+            p2q[h,:,cols]=y[:H]
+            p2s[h,1,:,cols]=y[H:2*H].astype(BF)
+            p2c[h,:,cols]=y[2*H:3*H]
+            p2s[h,0,:,cols]=y[3*H:].astype(BF)
+        def body(n,c):
+            part(pl.ds(pl.multiple_of(n*256,256),256))
+            return c
+        lax.fori_loop(0,D//256,body,0)
+        if D%256: part(pl.ds(D//256*256,D%256))
+        ds[h][0].start(); ds[h][1].start()
     wait_bytes(xh,xsem.at[1])
     xcopy=pltpu.make_async_copy(xh,x_o,osem); xcopy.start()
     scores_prep(xh,kk,vt)
+    zc[0].wait_recv(); zf[0].start()
     m=stage(0,xh,kk,vt,sa,None,None,None,None,first=True)
-    m=pairs(0,2,m)
-    c2.wait_recv(); c3.wait_recv()
-    pr=p1q[...]+p1r[1].astype(F32)+p1r[2].astype(F32)
-    rinv=lax.rsqrt(jnp.sum(pr*pr,axis=1,keepdims=True)+1e-6)
-    direction=pr*rinv
-    cosine=jnp.sum(direction*target,axis=1,keepdims=True)
-    ii=lax.broadcasted_iota(jnp.int32,(T,T),0); jj=lax.broadcasted_iota(jnp.int32,(T,T),1)
-    cos_o[...]=jnp.sum(jnp.where(ii==jj,cosine,0.0),axis=0,keepdims=True)
-    Z[0]=(-LOSS_WEIGHT*rinv*(target-cosine*direction)).astype(BF)
-    zc=[remote(Z.at[0,pl.ds(h*H,H)],Z.at[2,pl.ds(h*H,H)],zs.at[h],zr.at[h],cross) for h in range(2)]
-    zp=remote(Z.at[0],Z.at[1],zs.at[2],zr.at[2],partner)
-    zf=[remote(Z.at[2,pl.ds(h*H,H)],Z.at[3,pl.ds(h*H,H)],zs.at[3+h],zr.at[3+h],partner) for h in range(2)]
-    for c in zc: c.start()
-    zp.start()
-    zp.wait_recv()
-    def back(at,rows):
-        def body(n,c):
-            cols=pl.ds(pl.multiple_of(n*256,256),256)
-            gs=dot_nt(Z[at:at+2].reshape(2*T,C),wo[cols,:])
-            y=pre[pl.ds(rows,2*T),cols]
-            s=1.0/(1.0+jnp.exp(-y))
-            sil[pl.ds(rows,2*T),cols]=(gs*(s*(1.0+y*(1.0-s)))).astype(BF)
-            return c
-        lax.fori_loop(0,HID//256,body,0)
-    back(0,0)
-    m=pairs(2,3,m)
-    for h in range(2):
-        zc[h].wait_recv(); zf[h].start()
-        m=pairs(3+h,4+h,m)
-    for h in range(2): zf[h].wait_recv()
-    back(2,2*T)
-    def third(n,c):
-        cols=pl.ds(pl.multiple_of(n*128,128),128)
-        y=dot_nt(sil[2*T:],wi[cols,:])
-        p2c[:,cols]=y[:T]
-        p2s[0,:,cols]=y[T:].astype(BF)
-        return c
-    lax.fori_loop(0,D//128,third,0)
-    d1=remote(p2s.at[0],p2r.at[0],s2.at[0],r2.at[0],partner); d1.start()
-    def third_own(n,c):
-        cols=pl.ds(pl.multiple_of(n*128,128),128)
-        y=dot_nt(sil[:2*T],wi[cols,:])
-        p2q[:,cols]=y[:T]
-        p2s[1,:,cols]=y[T:].astype(BF)
-        return c
-    d1.wait_recv()
-    p2p[...]=(p2c[...]+p2r[0].astype(F32)).astype(BF)
-    d3=remote(p2p,p2r.at[2],s2.at[2],r2.at[2],cross); d3.start()
-    lax.fori_loop(0,D//128,third_own,0)
-    d2=remote(p2s.at[1],p2r.at[1],s2.at[1],r2.at[1],partner); d2.start()
-    m=pairs(5,7,m)
+    zc[1].wait_recv(); zf[1].start()
+    slope(0); third(0)
+    m=pairs(0,1,m)
+    pass_on(0,ds,p2c,p2r,p2p)
+    slope(1); third(1)
+    m=pairs(1,2,m)
+    pass_on(1,ds,p2c,p2r,p2p)
+    m=pairs(2,7,m)
     ucopy(0,0).wait()
     m=stage(NQ-1,xh,kk,vt,sb,sa,m,ua,a_o)
     ucopy(NQ-2,0).start()
-    ucopy(0,1).wait()
-    stage(NQ,xh,kk,vt,None,sb,m,ub,a_o,last=True)
-    ucopy(NQ-1,1).start()
     loads[2].wait()
-    d2.wait_recv(); d3.wait_recv()
-    gh=(cot[...].astype(F32)+(p2q[...]+p2r[1].astype(F32)+p2r[2].astype(F32))).astype(BF)
+    for h in range(2):
+        ds[h][1].wait_recv(); ds[h][2].wait_recv()
+        rows=pl.ds(h*H,H)
+        gh[rows]=(cot[rows].astype(F32)+(p2q[h]+p2r[h,1].astype(F32)+p2r[h,2].astype(F32))).astype(BF)
     R=512
     def heads(i,c):
         at=lax.rem(seq//8+i,L//2//R)
-        y=dot_nt(wa[pl.ds(pl.multiple_of(at*R,R),R)],Z2[...]).astype(BF)
+        y=dot_nt(wa[pl.ds(pl.multiple_of(at*R,R),R)],gh[...]).astype(BF)
         gt[pl.ds(at*8,8)]=y.reshape(8,HD,T)
         for e in range(8):
             h=at*8+lax.rem(seq+e,8)
@@ -273,12 +276,13 @@
             def _():
                 pltpu.make_async_copy(gt.at[h],g_o.at[seq],gsem.at[1]).start()
         return c
-    Z2=X.at[0]
-    X[0]=gh
     lax.fori_loop(0,4,heads,0)
+    ucopy(0,1).wait()
+    stage(NQ,xh,kk,vt,None,sb,m,ub,a_o,last=True)
+    ucopy(NQ-1,1).start()
     xcopy.wait()
     for n in range(2): ucopy(n,n).wait()
-    for c in hc+[hp]+hf+zc+[zp]+zf+[c1,c2,c3,d1,d2,d3]: c.wait_send()
+    for c in hc+hp+hf+zc+zp+zf+cs[0]+cs[1]+ds[0]+ds[1]: c.wait_send()
     wait_bytes(xt.at[pl.ds(0,NB-1)],xsem.at[0])
     wait_bytes(feat.at[pl.ds(0,NB-1)],fsem.at[0])
     wait_bytes(g_o,gsem.at[1]); wait_bytes(gt.at[pl.ds(0,NB-1)],gsem.at[0])
@@ -292,16 +296,17 @@
         out_shape=[jax.ShapeDtypeStruct((1,T),F32),jax.ShapeDtypeStruct((NB,3*HD,T),BF),jax.ShapeDtypeStruct((NB,HD,T),BF),
             jax.ShapeDtypeStruct((NQ,L,QB),BF),jax.ShapeDtypeStruct((HD+16,L),F32)],
         scratch_shapes=[V((D,HID),BF),V((HID,C),BF),V((2048,D),BF),V((NB,3*HD,T),BF),V((NB,HD,T),BF),V((NB,48,T),BF),
-            V((4,T,D),BF),V((4,T,C),BF),V((4*T,HID),F32),V((4*T,HID),BF),
-            V((2,T,C),BF),V((T,C),F32),V((T,C),BF),V((3,T,C),BF),V((T,C),F32),
-            V((2,T,D),BF),V((T,D),F32),V((T,D),BF),V((3,T,D),BF),V((T,D),F32),
+            V((2,4,T//2,D),BF),V((2,4,T//2,C),BF),V((2,2*T,HID),F32),V((2,2*T,HID),BF),
+            V((2,2,T//2,C),BF),V((2,T//2,C),F32),V((2,T//2,C),BF),V((2,3,T//2,C),BF),V((2,T//2,C),F32),
+            V((2,2,T//2,D),BF),V((2,T//2,D),F32),V((2,T//2,D),BF),V((2,3,T//2,D),BF),V((2,T//2,D),F32),
+            V((T,C),F32),V((T,D),BF),
             V((NB,3*HD,T),BF),V((L,T),BF),V((HD+16,L),BF),V((L,QB),F32),V((L,QB),F32),V((L,QB),BF),V((L,QB),BF),
-            S((3,)),S((2,)),S((2,)),S((2,)),S((5,)),S((5,)),S((5,)),S((5,)),S((3,)),S((3,)),S((3,)),S((3,)),S((2,)),S],
+            S((3,)),S((2,)),S((2,)),S((2,)),S((6,)),S((6,)),S((6,)),S((6,)),S((2,3)),S((2,3)),S((2,3)),S((2,3)),S((2,)),S],
         compiler_params=pltpu.CompilerParams(collective_id=0,has_side_effects=True,vmem_limit_bytes=62*2**20),
         name="front")(hid,cot,q,k,v,wi,wo,wa,dino)
 
 
-def finish_kernel(x_ref,g_ref,a_ref,u_h,q_o,k_o,v_o,vv,kt,ga,qn,gn,rlr,dq,u_ref,o_ref,buf,usem,ksem,qsem):
+def finish_kernel(x_ref,g_ref,a_ref,u_h,buf,vv,kt,ga,qn,gn,rlr,dq,u_ref,o_ref,usem,ksem,qsem):
     dp=lax.axis_index("dp"); seq=lax.axis_index("seq")
     NK=L//KB; per=KB//T
     first=seq//per
@@ -350,15 +355,8 @@
         give(lax.rem(seq+r,NB),pl.ds(0,HD),qsem)
         return c
     lax.fori_loop(0,NB,send,0)
-    kpart=buf.at[:,pl.ds(HD,2*HD)]
-    wait_bytes(kpart,ksem.at[1])
-    def out(ref,n):
-        for p in range(NB//2):
-            ref[:,p*T:(p+1)*T]=buf[2*p:2*p+2,n*HD:(n+1)*HD].reshape(T,T).T
-    out(k_o,1); out(v_o,2)
-    qpart=buf.at[:,pl.ds(0,HD)]
-    wait_bytes(qpart,qsem.at[1])
-    out(q_o,0)
+    wait_bytes(buf.at[:,pl.ds(HD,2*HD)],ksem.at[1])
+    wait_bytes(buf.at[:,pl.ds(0,HD)],qsem.at[1])
     wait_bytes(buf.at[pl.ds(0,NB-1),pl.ds(HD,2*HD)],ksem.at[0])
     wait_bytes(buf.at[pl.ds(0,NB-1),pl.ds(0,HD)],qsem.at[0])
 
@@ -366,17 +364,31 @@
 def finish(x,g,u,a):
     V=pltpu.VMEM; S=pltpu.SemaphoreType.DMA
     vm=pl.BlockSpec(memory_space=V); hb=pl.BlockSpec(memory_space=pl.ANY)
-    return pl.pallas_call(finish_kernel,in_specs=[vm]*3+[hb],out_specs=[vm]*3,
-        out_shape=[jax.ShapeDtypeStruct((T,NB*HD),BF)]*3,
+    return pl.pallas_call(finish_kernel,in_specs=[vm]*3+[hb],out_specs=vm,
+        out_shape=jax.ShapeDtypeStruct((NB,3*HD,T),BF),
         scratch_shapes=[V((L,T),BF),V((HD,L),BF),V((T,L),BF),V((L,HD),BF),V((L,HD),BF),V((8,L),F32),V((HD,L),F32),
-            V((2,NQ,KB,QB),BF),V((NB,3*HD,T),BF),V((NB,3*HD,T),BF),S((2,)),S((2,)),S((2,))],
+            V((2,NQ,KB,QB),BF),V((NB,3*HD,T),BF),S((2,)),S((2,)),S((2,))],
         compiler_params=pltpu.CompilerParams(collective_id=1,has_side_effects=True,vmem_limit_bytes=56*2**20),
         name="finish")(x,g,a,u)
 
 
+def place_kernel(o_ref,q_o,k_o,v_o):
+    for n,ref in enumerate((q_o,k_o,v_o)):
+        for p in range(o_ref.shape[0]//2):
+            ref[:,p*T:(p+1)*T]=o_ref[2*p:2*p+2,n*HD:(n+1)*HD].reshape(T,T).T
+
+
+def place(o):
+    steps=2
+    return pl.pallas_call(place_kernel,grid=(steps,),
+        in_specs=[pl.BlockSpec((NB//steps,3*HD,T),lambda i:(i,0,0))],
+        out_specs=[pl.BlockSpec((T,NB*HD//steps),lambda i:(0,i))]*3,
+        out_shape=[jax.ShapeDtypeStruct((T,NB*HD),BF)]*3,name="place")(o)
+
+
 def on_device(hidden,out_cot,proj_in,proj_out,attn_out_w,queries,keys,values,dino):
     cosine,x,g,u,a=front(hidden[0],out_cot[0],queries[0],keys[0],values[0],proj_in,proj_out,attn_out_w,dino[0])
-    gq,gk,gv=finish(x,g,u,a)
+    gq,gk,gv=place(finish(x,g,u,a))
     return cosine,gq[None],gk[None],gv[None]
 
 

time: 154 us -> 141 us (0.916)
  Pallas kernels: 147 us -> 139 us
  local copies, waits for them, and re-layouts: 6.16 us -> 0.51 us
    pallas_call x1, Pallas kernels: 95.5 us -> 85.5 us  [front(): pl.pallas_call(front_kernel, in_specs=[vm] * 5 + [hb] * 3 + [vm], out_spe...]
    unnamed x6 -> x3, local copies, waits for them, and re-layouts: 6.16 us -> 0.51 us
    pallas_call x1 -> x2, Pallas kernels: 51.1 us -> 53.8 us  [the longest x1 51.3 us: finish(): pl.pallas_call(finish_kernel, in_specs=[vm] * 3 + [hb], out_specs=vm, out...]
where the time goes in v4:
time: 141 us
  Pallas kernels  139 us (99%)
    pallas_call x1, Pallas kernels, front(): pl.pallas_call(front_kernel, in_specs=[vm] * 5 + [hb] * 3 + [vm], out_spe...  85.5 us
    pallas_call x1, Pallas kernels, finish(): pl.pallas_call(finish_kernel, in_specs=[vm] * 3 + [hb], out_specs=vm, out...  51.3 us

profile of v4, /device:TPU:0, one launch (start us, length us, event | category | flops | bytes accessed | tf_op | source)
XLA Modules:
  0.0 140.5 jit_solution(6172911245047120014)
XLA Ops:
  0.6 85.5 %front.1 = (f32[1,128]{1,0:T(1,128)}, bf16[32,192,128]{2,1,0:T(8,128)(2,1)}, bf16[32,64,128]{2,1,0:T(8,128)(2,1)}, bf16[16,4096,256]{2,1,0:T(8,128)(2,1)}, f32[80,4096]{1,0:T(8,128)}) custom-call(bf16[128,2432]{1,0:T(8,128)(2,1)} %bitcast.9, bf16[128,2432]{1,0:T(8,128)(2,1)} %bitcast.10, bf16[128,2048]{1,0:T(8,128)(2,1)} %bitcast.11, ...), custom_call_target="tpu_custom_call" | custom-call | tf_op jit(solution)/shard_map/front/pallas_call | solution.py:294
  86.2 0.0 copy-start
  86.2 51.3 %finish.1.o_ref = bf16[32,192,128]{2,1,0:T(8,128)(2,1)} custom-call(bf16[32,192,128]{2,1,0:T(8,128)(2,1)} %get-tuple-element.13.x_ref, bf16[32,64,128]{2,1,0:T(8,128)(2,1)} %get-tuple-element.14.g_ref, f32[80,4096]{1,0:T(8,128)} %get-tuple-element.15.a_ref, bf16[16,4096,256]{2,1,0:T(8,128)(2,1)} %get-tuple-element.16.u_h), custom_call_target="tpu_custom_call" | custom-call | tf_op jit(solution)/shard_map/finish/pallas_call | solution.py:367
  137.5 2.5 %place.1 = (bf16[128,2048]{1,0:T(8,128)(2,1)}, bf16[128,2048]{1,0:T(8,128)(2,1)}, bf16[128,2048]{1,0:T(8,128)(2,1)}) custom-call(bf16[32,192,128]{2,1,0:T(8,128)(2,1)} %finish.1.o_ref), custom_call_target="tpu_custom_call" | custom-call | tf_op jit(solution)/shard_map/place/pallas_call | solution.py:383
  140.0 0.0 copy-done
  140.0 0.5 copy.14
Async XLA Ops:
  86.2 53.8 %copy-start = (f32[1,128]{1,0:T(1,128)S(1)}, f32[1,128]{1,0:T(1,128)}, u32[]{:S(2)}) copy-start(f32[1,128]{1,0:T(1,128)} %get-tuple-element.24) | copy-start | bytes 1540

commit v5 on v4

--- a/solution.py
+++ b/solution.py
@@ -50,11 +50,11 @@
     return jnp.max(mn,axis=0,keepdims=True)
 
 
-def grads_prep(x,g_ref,a_ref,vv,kt,ga,qn,gn,rlr):
+def grads_prep(lo,hi,x,g_ref,a_ref,vv,kt,ga,qn,gn,rlr):
     lane=lax.broadcasted_iota(jnp.int32,(T,HD),1)
     ones=jnp.where(lane<2,1.0,0.0).astype(BF)
     row=lax.broadcasted_iota(jnp.int32,(HD,T),0)
-    for j in range(NB):
+    for j in range(lo,hi):
         rows=pl.ds(j*T,T)
         vv[rows,:]=jnp.concatenate([x[j,2*HD:].T,ones],axis=1)
         kt[:,rows]=x[j,HD:2*HD]*BF(0.125)
@@ -253,10 +253,7 @@
     slope(1); third(1)
     m=pairs(1,2,m)
     pass_on(1,ds,p2c,p2r,p2p)
-    m=pairs(2,7,m)
-    ucopy(0,0).wait()
-    m=stage(NQ-1,xh,kk,vt,sb,sa,m,ua,a_o)
-    ucopy(NQ-2,0).start()
+    m=pairs(2,4,m)
     loads[2].wait()
     for h in range(2):
         ds[h][1].wait_recv(); ds[h][2].wait_recv()
@@ -277,6 +274,10 @@
                 pltpu.make_async_copy(gt.at[h],g_o.at[seq],gsem.at[1]).start()
         return c
     lax.fori_loop(0,4,heads,0)
+    m=pairs(4,7,m)
+    ucopy(0,0).wait()
+    m=stage(NQ-1,xh,kk,vt,sb,sa,m,ua,a_o)
+    ucopy(NQ-2,0).start()
     ucopy(0,1).wait()
     stage(NQ,xh,kk,vt,None,sb,m,ub,a_o,last=True)
     ucopy(NQ-1,1).start()
@@ -310,15 +311,15 @@
     dp=lax.axis_index("dp"); seq=lax.axis_index("seq")
     NK=L//KB; per=KB//T
     first=seq//per
-    def place(b): return lax.rem(b+first,NK)
+    way=1-2*lax.rem(seq,2)
+    def place(b): return lax.rem(first+way*(b+1)+2*NK,NK)
     def fetch(b):
         slot=lax.rem(b,2)
         return pltpu.make_async_copy(u_h.at[:,pl.ds(pl.multiple_of(place(b)*KB,KB),KB)],u_ref.at[slot],usem.at[slot])
     fetch(0).start()
     greet(dp,seq,())
-    grads_prep(x_ref,g_ref,a_ref,vv,kt,ga,qn,gn,rlr)
-    dq[...]=jnp.zeros_like(dq)
-    meet(0)
+    def prep(i):
+        grads_prep(i*QP//T,(i+1)*QP//T,x_ref,g_ref,a_ref,vv,kt,ga,qn,gn,rlr)
     def give(h,part,sem):
         @pl.when(h!=seq)
         def _():
@@ -326,29 +327,43 @@
         @pl.when(h==seq)
         def _():
             pltpu.make_async_copy(o_ref.at[h,part],buf.at[seq,part],sem.at[1]).start()
+    def block(b,at,v,k,start):
+        slot=lax.rem(b,2)
+        dk=jnp.zeros((KB,HD),F32); dv=jnp.zeros((KB,HD),F32)
+        for i in range(L//QP):
+            if start and i+1<L//QP: prep(i+1)
+            qr=pl.ds(i*QP,QP)
+            n=QP//QB
+            u=jnp.concatenate([u_ref[slot,i*n+e] for e in range(n)],axis=1)
+            ds=(u.astype(F32)*dot(v,ga[:,qr])).astype(BF)
+            dk=dk+dot(ds,qn[qr,:]); dv=dv+dot(u,gn[qr,:])
+            part=dot(k,ds)
+            if start: dq[:,qr]=part
+            else: dq[:,qr]+=part
+        for j in range(per):
+            o_ref[at*per+j,HD:2*HD]=dk[j*T:(j+1)*T].T.astype(BF)
+            o_ref[at*per+j,2*HD:]=dv[j*T:(j+1)*T].T.astype(BF)
+        if start: meet(0)
+        for j in range(per):
+            give(at*per+lax.rem(seq+j,per),pl.ds(HD,2*HD),ksem)
+    prep(0)
+    at=place(0)
+    lane=lax.broadcasted_iota(jnp.int32,(T,HD),1)
+    ones=jnp.where(lane<2,1.0,0.0).astype(BF)
+    v=jnp.concatenate([jnp.concatenate([x_ref[at*per+j,2*HD:].T,ones],axis=1) for j in range(per)],axis=0)
+    k=jnp.concatenate([x_ref[at*per+j,HD:2*HD]*BF(0.125) for j in range(per)],axis=1)
+    fetch(1).start()
+    fetch(0).wait()
+    block(0,at,v,k,True)
     def body(b,c):
-        slot=lax.rem(b,2)
         @pl.when(b<NK-1)
         def _(): fetch(b+1).start()
         fetch(b).wait()
         at=place(b)
         kr=pl.ds(pl.multiple_of(at*KB,KB),KB)
-        v=vv[kr,:]; k=kt[:,kr]
-        dk=jnp.zeros((KB,HD),F32); dv=jnp.zeros((KB,HD),F32)
-        for i in range(L//QP):
-            qr=pl.ds(i*QP,QP)
-            n=QP//QB
-            u=jnp.concatenate([u_ref[slot,i*n+e] for e in range(n)],axis=1)
-            ds=(u.astype(F32)*dot(v,ga[:,qr])).astype(BF)
-            dk=dk+dot(ds,qn[qr,:]); dv=dv+dot(u,gn[qr,:])
-            dq[:,qr]+=dot(k,ds)
-        for j in range(per):
-            o_ref[at*per+j,HD:2*HD]=dk[j*T:(j+1)*T].T.astype(BF)
-            o_ref[at*per+j,2*HD:]=dv[j*T:(j+1)*T].T.astype(BF)
-        for j in range(per):
-            give(at*per+lax.rem(seq+j,per),pl.ds(HD,2*HD),ksem)
-        return c
-    lax.fori_loop(0,NK,body,0)
+        block(b,at,vv[kr,:],kt[:,kr],False)
+        return c
+    lax.fori_loop(1,NK,body,0)
     for j in range(NB):
         o_ref[j,:HD]=(dq[:,j*T:(j+1)*T]*rlr[0:1,j*T:(j+1)*T]).astype(BF)
     def send(r,c):

time: 141 us -> 138 us (0.979)
  Pallas kernels: 139 us -> 136 us
    pallas_call x1, Pallas kernels: 51.3 us -> 46.2 us  [finish(): pl.pallas_call(finish_kernel, in_specs=[vm] * 3 + [hb], out_specs=vm, out...]
    pallas_call x1, Pallas kernels: 85.5 us -> 87 us  [front(): pl.pallas_call(front_kernel, in_specs=[vm] * 5 + [hb] * 3 + [vm], out_spe...]
where the time goes in v5:
time: 138 us; the launch traced here: 137 us
  Pallas kernels  136 us (99%)
    pallas_call x1, Pallas kernels, front(): pl.pallas_call(front_kernel, in_specs=[vm] * 5 + [hb] * 3 + [vm], out_spe...  87 us
    pallas_call x1, Pallas kernels, finish(): pl.pallas_call(finish_kernel, in_specs=[vm] * 3 + [hb], out_specs=vm, out...  46.2 us

profile of v5, /device:TPU:0, one launch (start us, length us, event | category | flops | bytes accessed | tf_op | source)
XLA Modules:
  0.0 136.9 jit_solution(5295743358114126823)
XLA Ops:
  0.6 87.0 %front.1 = (f32[1,128]{1,0:T(1,128)}, bf16[32,192,128]{2,1,0:T(8,128)(2,1)}, bf16[32,64,128]{2,1,0:T(8,128)(2,1)}, bf16[16,4096,256]{2,1,0:T(8,128)(2,1)}, f32[80,4096]{1,0:T(8,128)}) custom-call(bf16[128,2432]{1,0:T(8,128)(2,1)} %bitcast.9, bf16[128,2432]{1,0:T(8,128)(2,1)} %bitcast.10, bf16[128,2048]{1,0:T(8,128)(2,1)} %bitcast.11, ...), custom_call_target="tpu_custom_call" | custom-call | tf_op jit(solution)/shard_map/front/pallas_call | solution.py:295
  87.6 0.0 copy-start
  87.6 46.2 %finish.1.o_ref = bf16[32,192,128]{2,1,0:T(8,128)(2,1)} custom-call(bf16[32,192,128]{2,1,0:T(8,128)(2,1)} %get-tuple-element.13.x_ref, bf16[32,64,128]{2,1,0:T(8,128)(2,1)} %get-tuple-element.14.g_ref, f32[80,4096]{1,0:T(8,128)} %get-tuple-element.15.a_ref, bf16[16,4096,256]{2,1,0:T(8,128)(2,1)} %get-tuple-element.16.u_h), custom_call_target="tpu_custom_call" | custom-call | tf_op jit(solution)/shard_map/finish/pallas_call | solution.py:382
  133.9 2.5 %place.1 = (bf16[128,2048]{1,0:T(8,128)(2,1)}, bf16[128,2048]{1,0:T(8,128)(2,1)}, bf16[128,2048]{1,0:T(8,128)(2,1)}) custom-call(bf16[32,192,128]{2,1,0:T(8,128)(2,1)} %finish.1.o_ref), custom_call_target="tpu_custom_call" | custom-call | tf_op jit(solution)/shard_map/place/pallas_call | solution.py:398
  136.4 0.0 copy-done
  136.4 0.5 copy.14
Async XLA Ops:
  87.6 48.7 %copy-start = (f32[1,128]{1,0:T(1,128)S(1)}, f32[1,128]{1,0:T(1,128)}, u32[]{:S(2)}) copy-start(f32[1,128]{1,0:T(1,128)} %get-tuple-element.24) | copy-start | bytes 1540

commit v6 on v5

--- a/solution.py
+++ b/solution.py
@@ -253,7 +253,7 @@
     slope(1); third(1)
     m=pairs(1,2,m)
     pass_on(1,ds,p2c,p2r,p2p)
-    m=pairs(2,4,m)
+    m=pairs(2,5,m)
     loads[2].wait()
     for h in range(2):
         ds[h][1].wait_recv(); ds[h][2].wait_recv()
@@ -274,7 +274,7 @@
                 pltpu.make_async_copy(gt.at[h],g_o.at[seq],gsem.at[1]).start()
         return c
     lax.fori_loop(0,4,heads,0)
-    m=pairs(4,7,m)
+    m=pairs(5,7,m)
     ucopy(0,0).wait()
     m=stage(NQ-1,xh,kk,vt,sb,sa,m,ua,a_o)
     ucopy(NQ-2,0).start()

time: 138 us -> 136 us (0.986)
  Pallas kernels: 136 us -> 134 us
    pallas_call x1, Pallas kernels: 87 us -> 84.8 us  [front(): pl.pallas_call(front_kernel, in_specs=[vm] * 5 + [hb] * 3 + [vm], out_spe...]
where the time goes in v6:
time: 136 us; the launch traced here: 135 us
  Pallas kernels  134 us (99%)
    pallas_call x1, Pallas kernels, front(): pl.pallas_call(front_kernel, in_specs=[vm] * 5 + [hb] * 3 + [vm], out_spe...  84.8 us
    pallas_call x1, Pallas kernels, finish(): pl.pallas_call(finish_kernel, in_specs=[vm] * 3 + [hb], out_specs=vm, out...  46.5 us

profile of v6, /device:TPU:0, one launch (start us, length us, event | category | flops | bytes accessed | tf_op | source)
XLA Modules:
  0.0 135.0 jit_solution(3660751061794899152)
XLA Ops:
  0.6 84.8 %front.1 = (f32[1,128]{1,0:T(1,128)}, bf16[32,192,128]{2,1,0:T(8,128)(2,1)}, bf16[32,64,128]{2,1,0:T(8,128)(2,1)}, bf16[16,4096,256]{2,1,0:T(8,128)(2,1)}, f32[80,4096]{1,0:T(8,128)}) custom-call(bf16[128,2432]{1,0:T(8,128)(2,1)} %bitcast.9, bf16[128,2432]{1,0:T(8,128)(2,1)} %bitcast.10, bf16[128,2048]{1,0:T(8,128)(2,1)} %bitcast.11, ...), custom_call_target="tpu_custom_call" | custom-call | tf_op jit(solution)/shard_map/front/pallas_call | solution.py:295
  85.4 0.0 copy-start
  85.4 46.5 %finish.1.o_ref = bf16[32,192,128]{2,1,0:T(8,128)(2,1)} custom-call(bf16[32,192,128]{2,1,0:T(8,128)(2,1)} %get-tuple-element.13.x_ref, bf16[32,64,128]{2,1,0:T(8,128)(2,1)} %get-tuple-element.14.g_ref, f32[80,4096]{1,0:T(8,128)} %get-tuple-element.15.a_ref, bf16[16,4096,256]{2,1,0:T(8,128)(2,1)} %get-tuple-element.16.u_h), custom_call_target="tpu_custom_call" | custom-call | tf_op jit(solution)/shard_map/finish/pallas_call | solution.py:382
  132.0 2.5 %place.1 = (bf16[128,2048]{1,0:T(8,128)(2,1)}, bf16[128,2048]{1,0:T(8,128)(2,1)}, bf16[128,2048]{1,0:T(8,128)(2,1)}) custom-call(bf16[32,192,128]{2,1,0:T(8,128)(2,1)} %finish.1.o_ref), custom_call_target="tpu_custom_call" | custom-call | tf_op jit(solution)/shard_map/place/pallas_call | solution.py:398
  134.5 0.0 copy-done
  134.5 0.5 copy.14
Async XLA Ops:
  85.4 49.0 %copy-start = (f32[1,128]{1,0:T(1,128)S(1)}, f32[1,128]{1,0:T(1,128)}, u32[]{:S(2)}) copy-start(f32[1,128]{1,0:T(1,128)} %get-tuple-element.24) | copy-start | bytes 1540
